TPU v7x, 256 devices: a whole 4x4x8 slice. The times are simulated.
256 devices in a mesh: row: 32 (over z, y_hi, core), col: 8 (over x, y_lo).
Axes of the slice: x: 4, y: 4 (y_hi: 2, y_lo: 2; y = y_hi * 2 + y_lo), z: 8, core: 2. Of those that a mesh axis runs over, the one named last changes fastest.
Arguments:
- left_blocks: bfloat16 [128, 64, 128, 128], P('row', 'col'), may hold values from -0.25 to 0.25
- left_index: int32 [128, 64], P('row', 'col'), may hold values from 0 to 3, as said below
- left_count: int32 [128, 32], P('row', 'col'), may hold values from 0 to 2
- right_blocks: bfloat16 [128, 24, 128, 128], P('row', 'col'), may hold values from -6 to 6
- right_index: int32 [128, 24], P('row', 'col'), may hold values from 0 to 15, as said below
- right_count: int32 [128, 8], P('row', 'col'), may hold values from 0 to 3
- product_index: int32 [128, 48], P('row', 'col'), may hold values from 0 to 15, as said below
- product_count: int32 [128, 8], P('row', 'col'), may hold values from 1 to 6
Outputs:
- product_blocks: float32 [128, 48, 128, 128], P('row', 'col')
Inputs may be any that keep to these rules, and one draw needn't show every extreme that they name: `left_index`: within one block row and one range, the 2 indices of the slots are distinct, dead slots included. `right_index`: within one block row and one index of col, the 3 indices are distinct, dead slots included. `product_index`: within one block row and one index of col, the 6 indices are distinct, unused slots included.
All inputs are finite; a program needn't handle non-finite values.
Results may differ from a plain program's by a relative error of at most 0.0003.
Values may be sent and summed in bfloat16 or wider, within the bound.
A program may use at most 256 MiB of HBM per device.

v0:
```python
import jax
import jax.numpy as jnp
from jax import lax
from jax.sharding import PartitionSpec as P


def per_device(
    left_blocks,
    left_index,
    left_count,
    right_blocks,
    right_index,
    right_count,
    product_index,
    product_count,
):
    local_rows = left_blocks.shape[0]
    left_whole, index_whole, count_whole = (
        lax.all_gather(left_blocks, "col", axis=1, tiled=True),
        lax.all_gather(left_index, "col", axis=1, tiled=True),
        lax.all_gather(left_count, "col", axis=1, tiled=True),
    )
    range_total = count_whole.shape[1]
    per_range = index_whole.shape[1] // range_total
    right_width = right_blocks.shape[1]
    out_width = product_index.shape[1]
    out_live = jnp.arange(out_width, dtype=jnp.int32)[None, :] < product_count
    right_all, rindex_all, rcount_all = (
        lax.all_gather(right_blocks, "row", axis=0, tiled=True),
        lax.all_gather(right_index, "row", axis=0, tiled=True),
        lax.all_gather(right_count, "row", axis=0, tiled=True),
    )
    slot_order = jnp.arange(index_whole.shape[1], dtype=jnp.int32)
    right_order = jnp.arange(right_width, dtype=jnp.int32)

    def row_products(items):
        left_row, index_row, count_row, target, kept = items
        columns = slot_order // per_range * local_rows + index_row
        alive = slot_order % per_range < jnp.repeat(count_row, per_range)
        chosen = right_all[columns]
        right_alive = right_order[None, :] < rcount_all[columns]
        valid = alive[:, None] & right_alive
        partial_value = jnp.einsum(
            "sab,stbc->stac", left_row, chosen, preferred_element_type=jnp.float32
        )
        match = (
            (rindex_all[columns][:, :, None] == target[None, None, :])
            & valid[:, :, None]
            & kept[None, None, :]
        )
        return jnp.einsum(
            "stu,stac->uac",
            match.astype(jnp.float32),
            partial_value,
            precision=lax.Precision.HIGHEST,
        )

    result = lax.map(row_products, (left_whole, index_whole, count_whole, product_index, out_live))
    return result


def solution(mesh):
    return jax.shard_map(
        per_device,
        mesh=mesh,
        in_specs=(
            P("row", "col", None, None),
            P("row", "col"),
            P("row", "col"),
            P("row", "col", None, None),
            P("row", "col"),
            P("row", "col"),
            P("row", "col"),
            P("row", "col"),
        ),
        out_specs=P("row", "col", None, None),
        check_vma=False,
    )
```

profile of v0, /device:TPU:1, one launch (start us, length us, event | category | flops | bytes accessed | tf_op | source)
XLA Modules:
  0.0 483.8 jit_solution(16362148962761824018)
XLA Ops:
  6.5 0.7 all-gather.8.cloned.1.call-update
  7.3 0.7 all-gather.6.cloned.1.call-update
  8.0 0.8 copy.22
  8.8 20.4 %all-gather.2 = s32[8,4,4]{2,1,0:T(4,128)S(1)} all-gather(s32[1,4,4]{2,1,0:T(4,128)S(1)} %bitcast.79), channel_id=1, replica_groups=mesh['row'=32,'col'=8] {'col'}, dimensions={0}, use_global_device_ids=true | all-gather | bytes 576 | tf_op jit(solution)/shard_map/all_gather | solution.py:21
  29.3 36.2 %all-gather = s32[8,8,4]{1,2,0:T(4,128)S(1)} all-gather(s32[1,8,4]{1,2,0:T(4,128)} %bitcast.80), channel_id=1, replica_groups=mesh['row'=32,'col'=8] {'col'}, dimensions={0}, use_global_device_ids=true | all-gather | bytes 1152 | tf_op jit(solution)/shard_map/all_gather | solution.py:20
  65.5 1.3 dynamic-slice
  67.5 0.8 bitcast_dynamic-update-slice_fusion
  68.2 29.9 %all-reduce = s32[128]{0:T(128)S(1)} all-reduce(s32[128]{0:T(128)S(1)} %bitcast_dynamic-update-slice_fusion), channel_id=1, replica_groups=mesh['row'=32,'col'=8] {'row'}, use_global_device_ids=true, to_apply=%add | all-reduce | flops 128 | bytes 1024
  98.1 47.4 %all-gather.1 = s32[32,4,3]{2,1,0:T(4,128)S(1)} all-gather(s32[1,4,3]{2,1,0:T(4,128)} %bitcast.81), channel_id=1, replica_groups=mesh['row'=32,'col'=8] {'row'}, dimensions={0}, use_global_device_ids=true | all-gather | bytes 1584 | tf_op jit(solution)/shard_map/all_gather | solution.py:30
  145.6 0.7 iota_compare_fusion.1
  146.3 38.7 %all-gather.8.cloned.1.call-done = bf16[4,64,128,128]{3,2,1,0:T(8,128)(2,1)} async-done(((bf16[4,8,128,128]{3,2,1,0:T(8,128)(2,1)}), bf16[4,64,128,128]{3,2,1,0:T(8,128)(2,1)}) %all-gather.8.cloned.1.call-update) | async-done | bytes 8388624 | tf_op jit(solution)/shard_map/all_gather | solution.py:19
  185.0 126.0 %all-gather.6.cloned.1.call-done = bf16[128,3,128,128]{3,2,1,0:T(8,128)(2,1)} async-done(((bf16[4,3,128,128]{3,2,1,0:T(8,128)(2,1)}), bf16[128,3,128,128]{3,2,1,0:T(8,128)(2,1)}) %all-gather.6.cloned.1.call-update) | async-done | bytes 12582928 | tf_op jit(solution)/shard_map/all_gather | solution.py:29
  311.0 165.9 %while.16 = (s32[]{:T(128)}, f32[4,6,128,128]{3,2,1,0:T(8,128)}, s32[4,64]{1,0:T(4,128)S(1)}, s32[128,3]{1,0:T(8,128)S(1)}, s32[4,6]{1,0:T(4,128)}, /*index=5*/s...) while((s32[]{:T(128)}, f32[4,6,128,128]{3,2,1,0:T(8,128)}, ...), condition=%wide.region_1.2_spmd.clone.clone, body=%wide.region_0.1_spmd.clone.clone.sunk | while | flops 1031804928 | bytes 72495200 | solution.py:58
  311.1 0.7 fusion.45
  311.8 0.8 gather_fusion.2
  312.6 0.1 reshape.240
  312.8 0.6 gather_fusion.1
  313.4 8.6 %gather_fusion = bf16[64,3,128,128]{3,2,1,0:T(8,128)(2,1)} fusion(bf16[128,3,128,128]{3,2,1,0:T(8,128)(2,1)} %get-tuple-element.444, s32[1024]{0:T(1024)S(1)} %pad_clamp_fusion.2), kind=kCustom, calls=%fused_computation.2.clone.clone.1 | custom fusion | bytes 12583168 | tf_op jit(solution)/shard_map/while/body/eval_jaxpr/gather | solution.py:40
  322.1 9.7 %convolution_bitcast_fusion.4 = f32[64,3,128,128]{2,3,1,0:T(8,128)} fusion(bf16[64,3,128,128]{3,2,1,0:T(8,128)(2,1)} %gather_fusion, bf16[4,64,128,128]{3,2,1,0:T(8,128)(2,1)} %get-tuple-element.445, s32[]{:T(128)S(6)} %copy.42), kind=kOutput, calls=%fused_computation.8.clone.1 | convolution fusion | flops 805306368 | bytes 20971524 | tf_op jit(solution)/shard_map/while/body/eval_jaxpr/sab,stbc->stac/dot_general | solution.py:43
  331.8 12.8 %copy.36 = f32[64,3,128,128]{3,0,1,2:T(8,128)} copy(f32[64,3,128,128]{2,3,1,0:T(8,128)} %convolution_bitcast_fusion.4) | data formatting | bytes 25165824 | tf_op jit(solution)/shard_map/while/body/eval_jaxpr/sab,stbc->stac/transpose | solution.py:43
  344.6 7.1 %convolution_bitcast_fusion.5 = f32[1,6,128,128]{3,1,2,0:T(8,128)S(1)} fusion(f32[64,3,128,128]{3,0,1,2:T(8,128)} %copy.36, s32[64,3]{0,1:T(4,128)S(1)} %copy.37, s32[6]{0:T(128)S(1)} %fusion.45, pred[6]{0:T(512)(128)(4,1)S(1)} %dynamic-slice_bitcast_fusion.2, pred[64,3]{0,1:T(4,128)(4,1)S(1)} %fusion.48), kind=kOutput, calls=%fused_computation.11.clone.1 | convolution fusion | flops 226495872 | bytes 12977118 | tf_op jit(solution)/shard_map/while/body/eval_jaxpr/stu,stac->uac/dot_general | solution.py:51
  351.7 0.8 copy_dynamic-update-slice_fusion.2
  352.5 0.7 fusion.45
  353.3 0.8 gather_fusion.2
  354.1 0.1 reshape.240
  354.2 0.6 gather_fusion.1
  354.9 8.6 %gather_fusion = bf16[64,3,128,128]{3,2,1,0:T(8,128)(2,1)} fusion(bf16[128,3,128,128]{3,2,1,0:T(8,128)(2,1)} %get-tuple-element.444, s32[1024]{0:T(1024)S(1)} %pad_clamp_fusion.2), kind=kCustom, calls=%fused_computation.2.clone.clone.1 | custom fusion | bytes 12583168 | tf_op jit(solution)/shard_map/while/body/eval_jaxpr/gather | solution.py:40
  363.6 9.7 %convolution_bitcast_fusion.4 = f32[64,3,128,128]{2,3,1,0:T(8,128)} fusion(bf16[64,3,128,128]{3,2,1,0:T(8,128)(2,1)} %gather_fusion, bf16[4,64,128,128]{3,2,1,0:T(8,128)(2,1)} %get-tuple-element.445, s32[]{:T(128)S(6)} %copy.42), kind=kOutput, calls=%fused_computation.8.clone.1 | convolution fusion | flops 805306368 | bytes 20971524 | tf_op jit(solution)/shard_map/while/body/eval_jaxpr/sab,stbc->stac/dot_general | solution.py:43
  373.3 12.8 %copy.36 = f32[64,3,128,128]{3,0,1,2:T(8,128)} copy(f32[64,3,128,128]{2,3,1,0:T(8,128)} %convolution_bitcast_fusion.4) | data formatting | bytes 25165824 | tf_op jit(solution)/shard_map/while/body/eval_jaxpr/sab,stbc->stac/transpose | solution.py:43
  386.1 7.1 %convolution_bitcast_fusion.5 = f32[1,6,128,128]{3,1,2,0:T(8,128)S(1)} fusion(f32[64,3,128,128]{3,0,1,2:T(8,128)} %copy.36, s32[64,3]{0,1:T(4,128)S(1)} %copy.37, s32[6]{0:T(128)S(1)} %fusion.45, pred[6]{0:T(512)(128)(4,1)S(1)} %dynamic-slice_bitcast_fusion.2, pred[64,3]{0,1:T(4,128)(4,1)S(1)} %fusion.48), kind=kOutput, calls=%fused_computation.11.clone.1 | convolution fusion | flops 226495872 | bytes 12977118 | tf_op jit(solution)/shard_map/while/body/eval_jaxpr/stu,stac->uac/dot_general | solution.py:51
  393.2 0.8 copy_dynamic-update-slice_fusion.2
  394.0 0.7 fusion.45
  394.7 0.8 gather_fusion.2
  395.6 0.1 reshape.240
  395.7 0.6 gather_fusion.1
  396.4 8.6 %gather_fusion = bf16[64,3,128,128]{3,2,1,0:T(8,128)(2,1)} fusion(bf16[128,3,128,128]{3,2,1,0:T(8,128)(2,1)} %get-tuple-element.444, s32[1024]{0:T(1024)S(1)} %pad_clamp_fusion.2), kind=kCustom, calls=%fused_computation.2.clone.clone.1 | custom fusion | bytes 12583168 | tf_op jit(solution)/shard_map/while/body/eval_jaxpr/gather | solution.py:40
  405.1 9.7 %convolution_bitcast_fusion.4 = f32[64,3,128,128]{2,3,1,0:T(8,128)} fusion(bf16[64,3,128,128]{3,2,1,0:T(8,128)(2,1)} %gather_fusion, bf16[4,64,128,128]{3,2,1,0:T(8,128)(2,1)} %get-tuple-element.445, s32[]{:T(128)S(6)} %copy.42), kind=kOutput, calls=%fused_computation.8.clone.1 | convolution fusion | flops 805306368 | bytes 20971524 | tf_op jit(solution)/shard_map/while/body/eval_jaxpr/sab,stbc->stac/dot_general | solution.py:43
  414.8 12.8 %copy.36 = f32[64,3,128,128]{3,0,1,2:T(8,128)} copy(f32[64,3,128,128]{2,3,1,0:T(8,128)} %convolution_bitcast_fusion.4) | data formatting | bytes 25165824 | tf_op jit(solution)/shard_map/while/body/eval_jaxpr/sab,stbc->stac/transpose | solution.py:43
  427.6 7.1 %convolution_bitcast_fusion.5 = f32[1,6,128,128]{3,1,2,0:T(8,128)S(1)} fusion(f32[64,3,128,128]{3,0,1,2:T(8,128)} %copy.36, s32[64,3]{0,1:T(4,128)S(1)} %copy.37, s32[6]{0:T(128)S(1)} %fusion.45, pred[6]{0:T(512)(128)(4,1)S(1)} %dynamic-slice_bitcast_fusion.2, pred[64,3]{0,1:T(4,128)(4,1)S(1)} %fusion.48), kind=kOutput, calls=%fused_computation.11.clone.1 | convolution fusion | flops 226495872 | bytes 12977118 | tf_op jit(solution)/shard_map/while/body/eval_jaxpr/stu,stac->uac/dot_general | solution.py:51
  434.7 0.8 copy_dynamic-update-slice_fusion.2
  435.5 0.7 fusion.45
  436.2 0.8 gather_fusion.2
  437.2 0.6 gather_fusion.1
  437.9 8.6 %gather_fusion = bf16[64,3,128,128]{3,2,1,0:T(8,128)(2,1)} fusion(bf16[128,3,128,128]{3,2,1,0:T(8,128)(2,1)} %get-tuple-element.444, s32[1024]{0:T(1024)S(1)} %pad_clamp_fusion.2), kind=kCustom, calls=%fused_computation.2.clone.clone.1 | custom fusion | bytes 12583168 | tf_op jit(solution)/shard_map/while/body/eval_jaxpr/gather | solution.py:40
  446.5 9.7 %convolution_bitcast_fusion.4 = f32[64,3,128,128]{2,3,1,0:T(8,128)} fusion(bf16[64,3,128,128]{3,2,1,0:T(8,128)(2,1)} %gather_fusion, bf16[4,64,128,128]{3,2,1,0:T(8,128)(2,1)} %get-tuple-element.445, s32[]{:T(128)S(6)} %copy.42), kind=kOutput, calls=%fused_computation.8.clone.1 | convolution fusion | flops 805306368 | bytes 20971524 | tf_op jit(solution)/shard_map/while/body/eval_jaxpr/sab,stbc->stac/dot_general | solution.py:43
  456.3 12.8 %copy.36 = f32[64,3,128,128]{3,0,1,2:T(8,128)} copy(f32[64,3,128,128]{2,3,1,0:T(8,128)} %convolution_bitcast_fusion.4) | data formatting | bytes 25165824 | tf_op jit(solution)/shard_map/while/body/eval_jaxpr/sab,stbc->stac/transpose | solution.py:43
  469.1 7.1 %convolution_bitcast_fusion.5 = f32[1,6,128,128]{3,1,2,0:T(8,128)S(1)} fusion(f32[64,3,128,128]{3,0,1,2:T(8,128)} %copy.36, s32[64,3]{0,1:T(4,128)S(1)} %copy.37, s32[6]{0:T(128)S(1)} %fusion.45, pred[6]{0:T(512)(128)(4,1)S(1)} %dynamic-slice_bitcast_fusion.2, pred[64,3]{0,1:T(4,128)(4,1)S(1)} %fusion.48), kind=kOutput, calls=%fused_computation.11.clone.1 | convolution fusion | flops 226495872 | bytes 12977118 | tf_op jit(solution)/shard_map/while/body/eval_jaxpr/stu,stac->uac/dot_general | solution.py:51
  476.2 0.8 copy_dynamic-update-slice_fusion.2
  (40 shorter events, 1.1 us)
Async XLA Ops:
  6.5 178.5 %all-gather.8.cloned.1.call-start = ((), (), s32[]{:S(2)}) async-start(), calls=%async_computation.1 | async-start | bytes 9437184 | tf_op jit(solution)/shard_map/all_gather | solution.py:19
  7.3 303.8 %all-gather.6.cloned.1.call-start = ((), (), s32[]{:S(2)}) async-start(), calls=%async_computation | async-start | bytes 12976128 | tf_op jit(solution)/shard_map/all_gather | solution.py:29
Sparse Core Ops, SparseCore 0:
  9.1 175.8 all-gather.7
  187.8 123.1 all-gather.5
where the time goes:
time: 485 us; the launch traced here: 484 us
  waiting for transfers between devices  166 us (34%)
  blocking collectives  134 us (28%)
  local copies, waits for them, and re-layouts  101 us (21%)
  matrix products  67.3 us (14%)
  between operations  14.1 us (3%)
    all_gather x1, waiting for transfers between devices, per_device(): lax.all_gather(right_blocks, 'row', axis=0, tiled=True)  126 us
    transpose x4, local copies, waits for them, and re-layouts, row_products(): jnp.einsum('sab,stbc->stac', left_row, chosen, preferred_element_type=jnp...  51.2 us
    all_gather x1, blocking collectives, per_device(): lax.all_gather(right_index, 'row', axis=0, tiled=True)  47.4 us
    dot_general x4, matrix products, row_products(): jnp.einsum('sab,stbc->stac', left_row, chosen, preferred_element_type=jnp...  38.9 us
    all_gather x1, waiting for transfers between devices, per_device(): lax.all_gather(left_blocks, 'col', axis=1, tiled=True)  38.7 us
    all_gather x1, blocking collectives, per_device(): lax.all_gather(left_index, 'col', axis=1, tiled=True)  36.2 us
    gather x4, local copies, waits for them, and re-layouts, row_products(): chosen = right_all[columns]  34.6 us
    unnamed x1, blocking collectives  29.9 us
  transfers between devices with their start and end apart: 2, of which 2 were waited for; matrix products, arithmetic and copies ran while one was open for 1% of the time, Pallas kernels for 0%

commit v1 on v0

v1 whole, which is shorter than its diff:
```python
import functools

import jax
import jax.numpy as jnp
from jax import lax
from jax.experimental import pallas as pl
from jax.experimental.pallas import tpu as pltpu
from jax.sharding import PartitionSpec as P

MESH = pl.DeviceIdType.MESH
BLK = 128
NZ, NX = 8, 4
ROWS, LSLOT, RSLOT, OSLOT = 4, 8, 3, 6
RDEV = ROWS * RSLOT
GROUP = 4 * RDEV
ZERO = GROUP


def kernel(lidx, lcnt, ridx, rcnt, pidx, pcnt, left, right, out, lbuf, *rest):
    rg = rest[:NZ]
    rm, rs, rc, lm, ls, lc, code_v, code, lk, send, recv, local = rest[NZ:]
    row, col = lax.axis_index("row"), lax.axis_index("col")
    z, h, e = row // 4, (row // 2) % 2, row % 2
    x, y = col // 2, col % 2
    g = h * 2 + e

    def zdev(d):
        return (((z + d) % NZ) * 4 + g, col)

    def xdev(d):
        return (row, ((x + d) % NX) * 2 + y)

    hdev = (z * 4 + (1 - h) * 2 + e, col)
    edev = (z * 4 + h * 2 + (1 - e), col)
    ydev = (row, x * 2 + (1 - y))

    barrier = pltpu.get_barrier_semaphore()
    partners = [zdev(d) for d in range(1, NZ)] + [xdev(d) for d in range(1, NX)] + [hdev, edev, ydev]
    for dev in partners:
        pl.semaphore_signal(barrier, inc=1, device_id=dev, device_id_type=MESH)

    own_left = pltpu.make_async_copy(left, lbuf.at[col], local.at[0])
    own_left.start()
    own_right = pltpu.make_async_copy(right, rg[0].at[pl.ds(g * RDEV, RDEV)], local.at[1])
    own_right.start()

    sub = lax.broadcasted_iota(jnp.int32, (8, BLK), 0)
    lane = lax.broadcasted_iota(jnp.int32, (8, BLK), 1)
    table = jnp.zeros((8, BLK), jnp.int32)
    for j in range(ROWS):
        for t in range(RSLOT):
            value = jnp.where(t < rcnt[j, 0], ridx[j, t] + 1, 0)
            table = jnp.where((sub == t) & (lane == row * ROWS + j), value, table)
    rm[0] = table
    table = jnp.zeros((8, BLK), jnp.int32)
    for i in range(ROWS):
        for s in range(LSLOT):
            value = jnp.where(s % 2 < lcnt[i, s // 2], (col * 4 + s // 2) * ROWS + lidx[i, s] + 1, 0)
            table = jnp.where((sub == i) & (lane == col * LSLOT + s), value, table)
    lm[0] = table

    pl.semaphore_wait(barrier, len(partners))

    copies = {}

    def push(name, src, dst, dev):
        n = len(copies)
        copy = pltpu.make_async_remote_copy(
            src_ref=src,
            dst_ref=dst,
            send_sem=send.at[n],
            recv_sem=recv.at[n],
            device_id=dev,
            device_id_type=MESH,
        )
        copy.start()
        copies[name] = copy

    def arrived(*names):
        for name in names:
            copies[name].wait_recv()

    def rpart(d, hh, first=0, size=RDEV):
        return rg[d % NZ].at[pl.ds((hh * 2 + e) * RDEV + first, size)]

    def lpart(dx, yy, half=None):
        at = ((x + dx) % NX) * 2 + yy
        if half is None:
            return lbuf.at[at]
        return lbuf.at[at, pl.ds(2 * half, 2)]

    push("ma", rm.at[0], rm.at[1], edev)
    push("na", lm.at[0], lm.at[1], ydev)
    push("r+1o", right, rpart(-1, h), zdev(1))
    push("r-1o", right, rpart(1, h), zdev(-1))
    push("rh", right, rpart(0, h), hdev)
    push("l+1", left, lpart(0, y), xdev(1))
    push("l-1", left, lpart(0, y), xdev(-1))
    push("ly", left, lpart(0, y), ydev)
    push("e0o", right, rpart(0, h), edev)

    arrived("ma", "na")
    rs[...] = rm[0] + rm[1]
    ls[...] = lm[0] + lm[1]
    push("mb", rs, rm.at[2], hdev)
    for d in range(1, NX):
        push(f"nb{d}", ls, lc.at[d - 1], xdev(d))
    arrived("mb")
    rs2 = rm.at[3]
    rs2[...] = rs[...] + rm[2]
    for d in range(1, NZ):
        push(f"mc{d}", rs2, rc.at[d - 1], zdev(d))
    for ref in rg:
        ref[ZERO] = jnp.zeros((BLK, BLK), jnp.bfloat16)

    def hop(d, hh, tag):
        arrived(f"r+{d}{tag}", f"r-{d}{tag}")
        if d < 3:
            push(f"r+{d + 1}{tag}", rpart(-d, hh), rpart(-d - 1, hh), zdev(1))
            push(f"r-{d + 1}{tag}", rpart(d, hh), rpart(d + 1, hh), zdev(-1))
        else:
            push(f"r+4{tag}", rpart(-d, hh, 0, 6), rpart(4, hh, 0, 6), zdev(1))
            push(f"r-4{tag}", rpart(d, hh, 6, 6), rpart(4, hh, 6, 6), zdev(-1))
        push(f"e-{d}{tag}", rpart(-d, hh), rpart(-d, hh), edev)
        push(f"e+{d}{tag}", rpart(d, hh), rpart(d, hh), edev)

    def last(hh, tag):
        arrived(f"r+4{tag}", f"r-4{tag}")
        push(f"e4{tag}", rpart(4, hh), rpart(4, hh), edev)

    hop(1, h, "o")
    arrived("rh")
    push("r+1p", rpart(0, 1 - h), rpart(-1, 1 - h), zdev(1))
    push("r-1p", rpart(0, 1 - h), rpart(1, 1 - h), zdev(-1))
    push("e0p", rpart(0, 1 - h), rpart(0, 1 - h), edev)

    arrived(*[f"mc{d}" for d in range(1, NZ)], *[f"nb{d}" for d in range(1, NX)])
    right_table = rs2[...]
    for d in range(NZ - 1):
        right_table = right_table + rc[d]
    left_table = ls[...]
    for d in range(NX - 1):
        left_table = left_table + lc[d]
    lc[NX - 1] = jnp.where(left_table == 0, BLK, left_table - 1)
    wide_sub = lax.broadcasted_iota(jnp.int32, (ROWS * OSLOT, BLK), 0)
    wide_lane = lax.broadcasted_iota(jnp.int32, (ROWS * OSLOT, BLK), 1)
    wanted = jnp.full((ROWS * OSLOT, BLK), -1, jnp.int32)
    for i in range(ROWS):
        for u in range(OSLOT):
            value = jnp.where(u < pcnt[i, 0], pidx[i, u] + 1, -1)
            wanted = jnp.where(wide_sub == i * OSLOT + u, value, wanted)
    found = jnp.full((ROWS * OSLOT, BLK), ZERO, jnp.int32)
    for t in range(RSLOT):
        found = jnp.where(right_table[t : t + 1, :] == wanted, (wide_lane % 16) * RSLOT + t, found)
    code_v[:, :BLK] = found
    code_v[:, BLK:] = jnp.full((ROWS * OSLOT, BLK), ZERO, jnp.int32)
    to_code = pltpu.make_async_copy(code_v, code, local.at[2])
    to_code.start()
    to_lk = pltpu.make_async_copy(lc.at[NX - 1], lk, local.at[3])
    to_lk.start()

    hop(2, h, "o")
    arrived("ly", "l+1", "l-1")
    push("a+1", lpart(0, 1 - y, 0), lpart(0, 1 - y, 0), xdev(1))
    push("a-1", lpart(0, 1 - y, 0), lpart(0, 1 - y, 0), xdev(-1))
    push("b+1", lpart(-1, y, 1), lpart(-1, y, 1), ydev)
    push("b-1", lpart(1, y, 1), lpart(1, y, 1), ydev)
    push("l+2", lpart(-1, y, 0), lpart(-1, y, 0), xdev(1))
    push("l-2", lpart(1, y, 1), lpart(1, y, 1), xdev(-1))
    hop(1, 1 - h, "p")
    hop(3, h, "o")
    arrived("a+1", "a-1", "b+1", "b-1")
    push("a+2", lpart(-1, 1 - y, 0), lpart(-1, 1 - y, 0), xdev(1))
    push("b-2", lpart(1, 1 - y, 1), lpart(1, 1 - y, 1), xdev(-1))
    hop(2, 1 - h, "p")
    last(h, "o")
    hop(3, 1 - h, "p")
    last(1 - h, "p")
    arrived("l+2", "l-2", "a+2", "b-2")
    for tag in "op":
        arrived(f"e0{tag}")
        for d in range(1, 4):
            arrived(f"e-{d}{tag}", f"e+{d}{tag}")
        arrived(f"e4{tag}")
    own_left.wait()
    own_right.wait()
    to_code.wait()
    to_lk.wait()

    out[...] = jnp.zeros_like(out)
    for d in (0, 1, 7, 2, 6, 3, 5, 4):
        c = (z + d) % NZ

        def one_row(i, carry, ref=rg[d], c=c):
            ks = [lk[i, c * LSLOT + s] for s in range(LSLOT)]
            lhs = jnp.concatenate([lbuf[c, i, s] for s in range(LSLOT)], axis=1)
            for u in range(0, OSLOT, 2):
                rhs = jnp.concatenate(
                    [
                        jnp.concatenate([ref[code[i * OSLOT + u + n, ks[s]]] for n in range(2)], axis=1)
                        for s in range(LSLOT)
                    ],
                    axis=0,
                )
                part = jnp.dot(lhs, rhs, preferred_element_type=jnp.float32)
                out[i, u] += part[:, :BLK]
                out[i, u + 1] += part[:, BLK:]
            return carry

        lax.fori_loop(0, ROWS, one_row, 0)

    for copy in copies.values():
        copy.wait_send()


COPIES = 80


def per_device(
    left_blocks,
    left_index,
    left_count,
    right_blocks,
    right_index,
    right_count,
    product_index,
    product_count,
):
    smem = pl.BlockSpec(memory_space=pltpu.SMEM)
    hbm = pl.BlockSpec(memory_space=pl.ANY)
    meta = functools.partial(pltpu.VMEM, dtype=jnp.int32)
    return pl.pallas_call(
        kernel,
        out_shape=jax.ShapeDtypeStruct((ROWS, OSLOT, BLK, BLK), jnp.float32),
        in_specs=[smem] * 6 + [hbm] * 2,
        out_specs=pl.BlockSpec(memory_space=pltpu.VMEM),
        scratch_shapes=[pltpu.VMEM((8, ROWS, LSLOT, BLK, BLK), jnp.bfloat16)]
        + [pltpu.VMEM((GROUP + 1, BLK, BLK), jnp.bfloat16)] * NZ
        + [
            meta((4, 8, BLK)),
            meta((8, BLK)),
            meta((NZ - 1, 8, BLK)),
            meta((2, 8, BLK)),
            meta((8, BLK)),
            meta((NX, 8, BLK)),
            meta((ROWS * OSLOT, 2 * BLK)),
            pltpu.SMEM((ROWS * OSLOT, 2 * BLK), jnp.int32),
            pltpu.SMEM((8, BLK), jnp.int32),
            pltpu.SemaphoreType.DMA((COPIES,)),
            pltpu.SemaphoreType.DMA((COPIES,)),
            pltpu.SemaphoreType.DMA((4,)),
        ],
        compiler_params=pltpu.CompilerParams(
            collective_id=0, has_side_effects=True, vmem_limit_bytes=48 * 1024 * 1024
        ),
    )(
        left_index,
        left_count,
        right_index,
        right_count,
        product_index,
        product_count,
        left_blocks,
        right_blocks.reshape(RDEV, BLK, BLK),
    )


def solution(mesh):
    return jax.shard_map(
        per_device,
        mesh=mesh,
        in_specs=(
            P("row", "col", None, None),
            P("row", "col"),
            P("row", "col"),
            P("row", "col", None, None),
            P("row", "col"),
            P("row", "col"),
            P("row", "col"),
            P("row", "col"),
        ),
        out_specs=P("row", "col", None, None),
        check_vma=False,
    )
```

time: 485 us -> 121 us (0.25)
  waiting for transfers between devices: 166 us -> 0 us
  blocking collectives: 134 us -> 0 us
  Pallas kernels: 0 us -> 113 us
  local copies, waits for them, and re-layouts: 101 us -> 7.57 us
  matrix products: 67.3 us -> 0 us
  between operations: 14.1 us -> 0.02 us
    all_gather x2 -> x0, waiting for transfers between devices: 165 us -> none  [the longest x1 126 us: per_device(): lax.all_gather(right_blocks, 'row', axis=0, tiled=True)]
    pallas_call x0 -> x1, Pallas kernels: none -> 113 us  [per_device(): pl.pallas_call(kernel, out_shape=jax.ShapeDtypeStruct((ROWS, OSLOT, BLK,...]
    all_gather x3 -> x0, blocking collectives: 104 us -> none  [the longest x1 47.4 us: per_device(): lax.all_gather(right_index, 'row', axis=0, tiled=True)]
    dot_general x8 -> x0, matrix products: 67.3 us -> none  [the longest x4 38.9 us: row_products(): jnp.einsum('sab,stbc->stac', left_row, chosen, preferred_element_type=jnp...]
    transpose x4 -> x0, local copies, waits for them, and re-layouts: 51.2 us -> none  [row_products(): jnp.einsum('sab,stbc->stac', left_row, chosen, preferred_element_type=jnp...]
    gather x16 -> x0, local copies, waits for them, and re-layouts: 40.4 us -> none  [the longest x4 34.6 us: row_products(): chosen = right_all[columns]]
    unnamed x1 -> x0, blocking collectives: 29.9 us -> none
  transfers between devices with their start and end apart: 2 -> 0, of which waited for: 2 -> 0; matrix products, arithmetic and copies ran while one was open for 1% -> 0% of each run, Pallas kernels for 0% -> 0%
where the time goes in v1:
time: 121 us
  Pallas kernels  113 us (93%)
  local copies, waits for them, and re-layouts  7.57 us (6%)
    pallas_call x1, Pallas kernels, per_device(): pl.pallas_call(kernel, out_shape=jax.ShapeDtypeStruct((ROWS, OSLOT, BLK,...  113 us
    unnamed x15, local copies, waits for them, and re-layouts  7.57 us

profile of v1, /device:TPU:1, one launch (start us, length us, event | category | flops | bytes accessed | tf_op | source)
XLA Modules:
  0.0 121.0 jit_solution(14317228127173807322)
XLA Ops:
  0.0 0.7 copy.9.rcnt
  0.7 0.7 copy.10.pcnt
  1.5 0.0 copy-start
  1.5 1.2 %copy-done = bf16[4,8,128,128]{3,2,1,0:T(8,128)(2,1)S(1)} copy-done((bf16[4,8,128,128]{3,2,1,0:T(8,128)(2,1)S(1)}, bf16[4,8,128,128]{3,2,1,0:T(8,128)(2,1)}, u32[]{:S(2)}) %copy-start) | copy-done | bytes 1048600
  2.7 0.0 copy-start.1
  2.7 1.0 copy-done.1
  3.7 0.0 copy-start.2
  3.7 0.7 copy-done.2
  4.4 0.0 copy-start.3
  4.4 0.7 copy-done.3
  5.1 0.0 copy-start.4
  5.1 0.7 copy-done.4
  5.8 0.0 copy-start.5
  5.8 0.7 copy-done.5
  6.4 113.5 %shard_map.82 = f32[4,6,128,128]{3,2,1,0:T(8,128)S(1)} custom-call(s32[4,8]{1,0:T(4,128)S(1)} %copy-done.2, s32[4,4]{1,0:T(4,128)S(1)} %copy-done.3, s32[4,3]{1,0:T(4,128)S(1)} %copy-done.4, s32[4,1]{1,0:T(4,128)S(1)} %copy.9.rcnt, s32[4,6]{1,0:T(4,128)S(1)} %copy-done.5, s32[4,1]{1,0:T(4,128)S(1)} %copy.10.pcnt, bf16[4,8,128,128]{3,2,1,0:T(8,128)(2,1)S(1)} %copy-done, ...), custom_call_target="tpu_custom_call" | custom-call | tf_op jit(solution)/shard_map/pallas_call | solution.py:232
  119.9 1.1 copy.12
Async XLA Ops:
  1.5 1.2 %copy-start = (bf16[4,8,128,128]{3,2,1,0:T(8,128)(2,1)S(1)}, bf16[4,8,128,128]{3,2,1,0:T(8,128)(2,1)}, u32[]{:S(2)}) copy-start(bf16[4,8,128,128]{3,2,1,0:T(8,128)(2,1)} %left.1) | copy-start | bytes 3145732
  2.7 1.0 copy-start.1
  3.7 0.7 copy-start.2
  4.4 0.7 copy-start.3
  5.1 0.7 copy-start.4
  5.8 0.7 copy-start.5

commit v2 on v1

v2 whole, which is shorter than its diff:
```python
import functools

import jax
import jax.numpy as jnp
from jax import lax
from jax.experimental import pallas as pl
from jax.experimental.pallas import tpu as pltpu
from jax.sharding import PartitionSpec as P

MESH = pl.DeviceIdType.MESH
BLK = 128
NZ, NX = 8, 4
ROWS, LSLOT, RSLOT, OSLOT = 4, 8, 3, 6
RDEV = ROWS * RSLOT
ZERO = 4 * RDEV
GROUP = ZERO + 1
COPIES = 96


def kernel(*refs):
    small_in, (left, right, out, lbuf, early, mid, far), rest = refs[:6], refs[6:13], refs[13:]
    small, rest = rest[:6], rest[6:]
    lidx, lcnt, ridx, rcnt, pidx, pcnt = small
    rm, rs, rc, lm, ls, lc, code_v, code, lk, send, recv, local = rest
    row, col = lax.axis_index("row"), lax.axis_index("col")
    z, h, e = row // 4, (row // 2) % 2, row % 2
    x, y = col // 2, col % 2

    def zdev(d):
        return (((z + d) % NZ) * 4 + h * 2 + e, col)

    def xdev(d):
        return (row, ((x + d) % NX) * 2 + y)

    hdev = (z * 4 + (1 - h) * 2 + e, col)
    edev = (z * 4 + h * 2 + (1 - e), col)
    ydev = (row, x * 2 + (1 - y))

    barrier = pltpu.get_barrier_semaphore()
    partners = [zdev(1), zdev(-1), xdev(1), xdev(-1), hdev, edev, ydev]
    for dev in partners:
        pl.semaphore_signal(barrier, inc=1, device_id=dev, device_id_type=MESH)

    def rpart(d, hh, half=None):
        ref, group = (far, 0) if d in (4, -4) else (mid, (d + 3) // 6) if d in (3, -3) else (early, d + 2)
        first = group * GROUP + (hh * 2 + e) * RDEV
        if half is None:
            return ref.at[pl.ds(first, RDEV)]
        return ref.at[pl.ds(first + half * (RDEV // 2), RDEV // 2)]

    def lpart(dx, yy, half=None):
        at = ((x + dx) % NX) * 2 + yy
        if half is None:
            return lbuf.at[at]
        return lbuf.at[at, pl.ds(2 * half, 2)]

    loads = [pltpu.make_async_copy(a, b, local.at[n]) for n, (a, b) in enumerate(zip(small_in, small))]
    for load in loads:
        load.start()
    own_left = pltpu.make_async_copy(left, lpart(0, y), local.at[6])
    own_left.start()
    own_right = pltpu.make_async_copy(right, rpart(0, h), local.at[7])
    own_right.start()
    for load in loads:
        load.wait()

    sub = lax.broadcasted_iota(jnp.int32, (8, BLK), 0)
    lane = lax.broadcasted_iota(jnp.int32, (8, BLK), 1)
    table = jnp.zeros((8, BLK), jnp.int32)
    for j in range(ROWS):
        for t in range(RSLOT):
            value = jnp.where(t < rcnt[j], ridx[j, t] + 1, 0)
            table = jnp.where((sub == t) & (lane == row * ROWS + j), value, table)
    rm[0] = table
    table = jnp.zeros((8, BLK), jnp.int32)
    for i in range(ROWS):
        for s in range(LSLOT):
            value = jnp.where(s % 2 < lcnt[i, s // 2], (col * 4 + s // 2) * ROWS + lidx[i, s] + 1, 0)
            table = jnp.where((sub == i) & (lane == col * LSLOT + s), value, table)
    lm[0] = table

    pl.semaphore_wait(barrier, len(partners))

    copies = {}

    def push(name, src, dst, dev):
        n = len(copies)
        copy = pltpu.make_async_remote_copy(
            src_ref=src,
            dst_ref=dst,
            send_sem=send.at[n],
            recv_sem=recv.at[n],
            device_id=dev,
            device_id_type=MESH,
        )
        copy.start()
        copies[name] = copy

    def arrived(*names):
        for name in names:
            copies[name].wait_recv()

    def hop(d, hh, tag, half):
        arrived(f"r+{d}{tag}{half}", f"r-{d}{tag}{half}")
        if d < 3 or half == 0:
            push(f"r+{d + 1}{tag}{half}", rpart(-d, hh, half), rpart(-d - 1, hh, half), zdev(1))
        if d < 3 or half == 1:
            push(f"r-{d + 1}{tag}{half}", rpart(d, hh, half), rpart(d + 1, hh, half), zdev(-1))

    def share(d, hh, tag):
        push(f"e-{d}{tag}", rpart(-d, hh), rpart(-d, hh), edev)
        push(f"e+{d}{tag}", rpart(d, hh), rpart(d, hh), edev)

    push("ma", rm.at[0], rm.at[1], edev)
    push("na", lm.at[0], lm.at[1], ydev)
    for half in range(2):
        own = right.at[pl.ds(half * (RDEV // 2), RDEV // 2)]
        push(f"r+1o{half}", own, rpart(-1, h, half), zdev(1))
        push(f"r-1o{half}", own, rpart(1, h, half), zdev(-1))
    push("rh", right, rpart(0, h), hdev)
    push("l+1a", left.at[pl.ds(0, 2)], lpart(0, y, 0), xdev(1))
    push("l-1b", left.at[pl.ds(2, 2)], lpart(0, y, 1), xdev(-1))
    push("lya", left.at[pl.ds(0, 2)], lpart(0, y, 0), ydev)
    push("l+1b", left.at[pl.ds(2, 2)], lpart(0, y, 1), xdev(1))
    push("l-1a", left.at[pl.ds(0, 2)], lpart(0, y, 0), xdev(-1))
    push("lyb", left.at[pl.ds(2, 2)], lpart(0, y, 1), ydev)
    push("e0o", right, rpart(0, h), edev)

    out[...] = jnp.zeros_like(out)
    for ref, groups in ((early, 5), (mid, 2), (far, 1)):
        for group in range(groups):
            ref[group * GROUP + ZERO] = jnp.zeros((BLK, BLK), jnp.bfloat16)
    code_v[:, BLK:] = jnp.full((ROWS * OSLOT, BLK), ZERO, jnp.int32)
    arrived("ma", "na")
    rs[...] = rm[0] + rm[1]
    ls[...] = lm[0] + lm[1]
    push("mb", rs, rm.at[2], hdev)
    push("nb+1", ls, lc.at[0], xdev(1))
    push("nb-1", ls, lc.at[2], xdev(-1))

    hop(1, h, "o", 0)
    hop(1, h, "o", 1)
    share(1, h, "o")
    arrived("mb")
    rc[0] = rs[...] + rm[2]
    push("mc+1", rc.at[0], rc.at[7], zdev(1))
    push("mc-1", rc.at[0], rc.at[1], zdev(-1))
    arrived("rh")
    for half in range(2):
        push(f"r+1p{half}", rpart(0, 1 - h, half), rpart(-1, 1 - h, half), zdev(1))
        push(f"r-1p{half}", rpart(0, 1 - h, half), rpart(1, 1 - h, half), zdev(-1))
    push("e0p", rpart(0, 1 - h), rpart(0, 1 - h), edev)
    arrived("l+1a", "l-1b")
    push("b-1", lpart(1, y, 1), lpart(1, y, 1), ydev)
    hop(2, h, "o", 0)
    hop(2, h, "o", 1)
    share(2, h, "o")
    arrived("mc+1", "mc-1", "nb+1", "nb-1")
    push("mc+2", rc.at[7], rc.at[6], zdev(1))
    push("mc-2", rc.at[1], rc.at[2], zdev(-1))
    push("nb+2", lc.at[0], lc.at[1], xdev(1))
    arrived("lya")
    push("a+1", lpart(0, 1 - y, 0), lpart(0, 1 - y, 0), xdev(1))
    push("a-1", lpart(0, 1 - y, 0), lpart(0, 1 - y, 0), xdev(-1))
    hop(1, 1 - h, "p", 0)
    arrived("l+1b", "l-1a")
    push("l+2", lpart(-1, y, 0), lpart(-1, y, 0), xdev(1))
    push("l-2", lpart(1, y, 1), lpart(1, y, 1), xdev(-1))
    push("b+1", lpart(-1, y, 1), lpart(-1, y, 1), ydev)
    hop(1, 1 - h, "p", 1)
    share(1, 1 - h, "p")
    arrived("mc+2", "mc-2", "nb+2")
    push("mc+3", rc.at[6], rc.at[5], zdev(1))
    push("mc-3", rc.at[2], rc.at[3], zdev(-1))
    hop(3, h, "o", 0)
    hop(3, h, "o", 1)
    share(3, h, "o")
    arrived("mc+3", "mc-3")
    push("mc+4", rc.at[5], rc.at[4], zdev(1))
    arrived("a+1", "a-1")
    push("a+2", lpart(-1, 1 - y, 0), lpart(-1, 1 - y, 0), xdev(1))
    hop(2, 1 - h, "p", 0)
    hop(2, 1 - h, "p", 1)
    share(2, 1 - h, "p")
    arrived("lyb", "b-1")
    push("b-2", lpart(1, 1 - y, 1), lpart(1, 1 - y, 1), xdev(-1))

    arrived("mc+4")
    right_table = rc[0]
    for d in range(1, NZ):
        right_table = right_table + rc[d]
    left_table = ls[...]
    for d in range(NX - 1):
        left_table = left_table + lc[d]
    lc[NX - 1] = jnp.where(left_table == 0, BLK, left_table - 1)
    wide_sub = lax.broadcasted_iota(jnp.int32, (ROWS * OSLOT, BLK), 0)
    wide_lane = lax.broadcasted_iota(jnp.int32, (ROWS * OSLOT, BLK), 1)
    wanted = jnp.full((ROWS * OSLOT, BLK), -1, jnp.int32)
    for i in range(ROWS):
        for u in range(OSLOT):
            value = jnp.where(u < pcnt[i], pidx[i, u] + 1, -1)
            wanted = jnp.where(wide_sub == i * OSLOT + u, value, wanted)
    found = jnp.full((ROWS * OSLOT, BLK), ZERO, jnp.int32)
    for t in range(RSLOT):
        found = jnp.where(right_table[t : t + 1, :] == wanted, (wide_lane % 16) * RSLOT + t, found)
    code_v[:, :BLK] = found
    to_code = pltpu.make_async_copy(code_v, code, local.at[8])
    to_code.start()
    to_lk = pltpu.make_async_copy(lc.at[NX - 1], lk, local.at[9])
    to_lk.start()

    def multiply(ref, groups, d_of, rows_of):
        def one_group(j, carry):
            c = (z + d_of(j) + NZ) % NZ
            dx, dy = (c // 2 - x + NX) % NX, (c + y) % 2

            def one_row(i, carry):
                ks = [lk[i, c * LSLOT + s] for s in range(LSLOT)]
                lhs = jnp.concatenate([lbuf[c, i, s] for s in range(LSLOT)], axis=1)
                for u in range(0, OSLOT, 2):
                    rhs = jnp.concatenate(
                        [
                            jnp.concatenate(
                                [ref[j * GROUP + code[i * OSLOT + u + n, ks[s]]] for n in range(2)], axis=1
                            )
                            for s in range(LSLOT)
                        ],
                        axis=0,
                    )
                    part = jnp.dot(lhs, rhs, preferred_element_type=jnp.float32)
                    out[i, u] += part[:, :BLK]
                    out[i, u + 1] += part[:, BLK:]
                return carry

            first, last = rows_of(dx, dy)
            lax.fori_loop(first, last, one_row, 0)
            return carry

        lax.fori_loop(0, groups, one_group, 0)

    def early_d(j):
        return j - 2

    def mid_d(j):
        return 6 * j - 3

    def far_d(j):
        return 4

    def first_point(dx, dy):
        return jnp.where(dx == 2, 0, jnp.where((dx == 3) & (dy == 1), 2, 4))

    def second_point(dx, dy):
        return jnp.where((dx == 2) & (dy == 1), 0, 4)

    for tag in "op":
        arrived(f"e0{tag}")
        for d in range(1, 3):
            arrived(f"e-{d}{tag}", f"e+{d}{tag}")
    own_left.wait()
    own_right.wait()
    to_code.wait()
    to_lk.wait()
    multiply(early, 5, early_d, lambda dx, dy: (0, first_point(dx, dy)))

    arrived("r+4o0", "r-4o1")
    push("e4o", rpart(4, h), rpart(4, h), edev)
    hop(3, 1 - h, "p", 0)
    hop(3, 1 - h, "p", 1)
    share(3, 1 - h, "p")
    arrived("l+2", "l-2", "b+1")
    multiply(early, 5, early_d, lambda dx, dy: (first_point(dx, dy), second_point(dx, dy)))
    for tag in "op":
        arrived(f"e-3{tag}", f"e+3{tag}")
    multiply(mid, 2, mid_d, lambda dx, dy: (0, second_point(dx, dy)))
    arrived("r+4p0", "r-4p1")
    push("e4p", rpart(4, 1 - h), rpart(4, 1 - h), edev)
    arrived("a+2", "b-2")
    multiply(early, 5, early_d, lambda dx, dy: (second_point(dx, dy), 4))
    multiply(mid, 2, mid_d, lambda dx, dy: (second_point(dx, dy), 4))
    arrived("e4o", "e4p")
    multiply(far, 1, far_d, lambda dx, dy: (0, 4))

    for copy in copies.values():
        copy.wait_send()


def per_device(
    left_blocks,
    left_index,
    left_count,
    right_blocks,
    right_index,
    right_count,
    product_index,
    product_count,
):
    small = (
        left_index,
        left_count,
        right_index,
        right_count.reshape(ROWS),
        product_index,
        product_count.reshape(ROWS),
    )
    meta = functools.partial(pltpu.VMEM, dtype=jnp.int32)
    return pl.pallas_call(
        kernel,
        out_shape=jax.ShapeDtypeStruct((ROWS, OSLOT, BLK, BLK), jnp.float32),
        in_specs=[pl.BlockSpec(memory_space=pltpu.HBM)] * 8,
        out_specs=pl.BlockSpec(memory_space=pltpu.VMEM),
        scratch_shapes=[pltpu.VMEM((8, ROWS, LSLOT, BLK, BLK), jnp.bfloat16)]
        + [pltpu.VMEM((n * GROUP, BLK, BLK), jnp.bfloat16) for n in (5, 2, 1)]
        + [pltpu.SMEM(a.shape, jnp.int32) for a in small]
        + [
            meta((3, 8, BLK)),
            meta((8, BLK)),
            meta((NZ, 8, BLK)),
            meta((2, 8, BLK)),
            meta((8, BLK)),
            meta((NX, 8, BLK)),
            meta((ROWS * OSLOT, 2 * BLK)),
            pltpu.SMEM((ROWS * OSLOT, 2 * BLK), jnp.int32),
            pltpu.SMEM((8, BLK), jnp.int32),
            pltpu.SemaphoreType.DMA((COPIES,)),
            pltpu.SemaphoreType.DMA((COPIES,)),
            pltpu.SemaphoreType.DMA((10,)),
        ],
        compiler_params=pltpu.CompilerParams(
            collective_id=0, has_side_effects=True, vmem_limit_bytes=63 * 1024 * 1024
        ),
    )(*small, left_blocks, right_blocks.reshape(RDEV, BLK, BLK))


def solution(mesh):
    return jax.shard_map(
        per_device,
        mesh=mesh,
        in_specs=(
            P("row", "col", None, None),
            P("row", "col"),
            P("row", "col"),
            P("row", "col", None, None),
            P("row", "col"),
            P("row", "col"),
            P("row", "col"),
            P("row", "col"),
        ),
        out_specs=P("row", "col", None, None),
        check_vma=False,
    )
```

time: 121 us -> 98.2 us (0.81)
  Pallas kernels: 113 us -> 95.4 us
  local copies, waits for them, and re-layouts: 7.57 us -> 2.7 us
    pallas_call x1, Pallas kernels: 113 us -> 95.4 us  [per_device(): pl.pallas_call(kernel, out_shape=jax.ShapeDtypeStruct((ROWS, OSLOT, BLK,...]
    unnamed x15 -> x1, local copies, waits for them, and re-layouts: 7.57 us -> 2.7 us
where the time goes in v2:
time: 98.2 us; the launch traced here: 98.1 us
  Pallas kernels  95.4 us (97%)
  local copies, waits for them, and re-layouts  2.7 us (3%)
    pallas_call x1, Pallas kernels, per_device(): pl.pallas_call(kernel, out_shape=jax.ShapeDtypeStruct((ROWS, OSLOT, BLK,...  95.4 us
    unnamed x1, local copies, waits for them, and re-layouts  2.7 us

profile of v2, /device:TPU:1, one launch (start us, length us, event | category | flops | bytes accessed | tf_op | source)
XLA Modules:
  0.0 98.1 jit_solution(1893631444764747717)
XLA Ops:
  0.0 95.4 %shard_map.82 = f32[4,6,128,128]{3,2,1,0:T(8,128)} custom-call(s32[4,8]{1,0:T(4,128)} %refs_0_.1, s32[4,4]{1,0:T(4,128)} %refs_1_.1, s32[4,3]{1,0:T(4,128)} %refs_2_.1, s32[4]{0:T(128)} %bitcast.4, s32[4,6]{1,0:T(4,128)} %refs_4_.1, s32[4]{0:T(128)} %bitcast.5, bf16[4,8,128,128]{3,2,1,0:T(8,128)(2,1)} %refs_6_.1, bf16[12,128,128]{2,1,0:T(8,128)(2,1)} %bitcast.3), custom_call_target="tpu_custom_call" | custom-call | tf_op jit(solution)/shard_map/pallas_call | solution.py:307
  95.4 2.7 %copy.10 = f32[4,6,128,128]{3,2,1,0:T(8,128)} copy(f32[4,6,128,128]{3,2,1,0:T(8,128)} %shard_map.82) | data formatting | bytes 3145728

commit v3 on v2

--- a/solution.py
+++ b/solution.py
@@ -117,34 +117,37 @@
         own = right.at[pl.ds(half * (RDEV // 2), RDEV // 2)]
         push(f"r+1o{half}", own, rpart(-1, h, half), zdev(1))
         push(f"r-1o{half}", own, rpart(1, h, half), zdev(-1))
-    push("rh", right, rpart(0, h), hdev)
-    push("l+1a", left.at[pl.ds(0, 2)], lpart(0, y, 0), xdev(1))
-    push("l-1b", left.at[pl.ds(2, 2)], lpart(0, y, 1), xdev(-1))
-    push("lya", left.at[pl.ds(0, 2)], lpart(0, y, 0), ydev)
-    push("l+1b", left.at[pl.ds(2, 2)], lpart(0, y, 1), xdev(1))
-    push("l-1a", left.at[pl.ds(0, 2)], lpart(0, y, 0), xdev(-1))
-    push("lyb", left.at[pl.ds(2, 2)], lpart(0, y, 1), ydev)
-    push("e0o", right, rpart(0, h), edev)
-
-    out[...] = jnp.zeros_like(out)
-    for ref, groups in ((early, 5), (mid, 2), (far, 1)):
-        for group in range(groups):
-            ref[group * GROUP + ZERO] = jnp.zeros((BLK, BLK), jnp.bfloat16)
-    code_v[:, BLK:] = jnp.full((ROWS * OSLOT, BLK), ZERO, jnp.int32)
     arrived("ma", "na")
     rs[...] = rm[0] + rm[1]
     ls[...] = lm[0] + lm[1]
     push("mb", rs, rm.at[2], hdev)
     push("nb+1", ls, lc.at[0], xdev(1))
     push("nb-1", ls, lc.at[2], xdev(-1))
-
-    hop(1, h, "o", 0)
-    hop(1, h, "o", 1)
-    share(1, h, "o")
-    arrived("mb")
+    push("rh", right, rpart(0, h), hdev)
+    push("l+1a", left.at[pl.ds(0, 2)], lpart(0, y, 0), xdev(1))
+    push("l-1b", left.at[pl.ds(2, 2)], lpart(0, y, 1), xdev(-1))
+    push("lya", left.at[pl.ds(0, 2)], lpart(0, y, 0), ydev)
+    push("e0o", right, rpart(0, h), edev)
+    arrived("mb", "nb+1", "nb-1")
     rc[0] = rs[...] + rm[2]
     push("mc+1", rc.at[0], rc.at[7], zdev(1))
     push("mc-1", rc.at[0], rc.at[1], zdev(-1))
+    push("nb+2", lc.at[0], lc.at[1], xdev(1))
+    push("l+1b", left.at[pl.ds(2, 2)], lpart(0, y, 1), xdev(1))
+    push("l-1a", left.at[pl.ds(0, 2)], lpart(0, y, 0), xdev(-1))
+    push("lyb", left.at[pl.ds(2, 2)], lpart(0, y, 1), ydev)
+
+    hop(1, h, "o", 0)
+    out[...] = jnp.zeros_like(out)
+    for ref, groups in ((early, 5), (mid, 2), (far, 1)):
+        for group in range(groups):
+            ref[group * GROUP + ZERO] = jnp.zeros((BLK, BLK), jnp.bfloat16)
+    code_v[:, BLK:] = jnp.full((ROWS * OSLOT, BLK), ZERO, jnp.int32)
+    arrived("mc+1", "mc-1")
+    push("mc+2", rc.at[7], rc.at[6], zdev(1))
+    push("mc-2", rc.at[1], rc.at[2], zdev(-1))
+    hop(1, h, "o", 1)
+    share(1, h, "o")
     arrived("rh")
     for half in range(2):
         push(f"r+1p{half}", rpart(0, 1 - h, half), rpart(-1, 1 - h, half), zdev(1))
@@ -152,16 +155,17 @@
     push("e0p", rpart(0, 1 - h), rpart(0, 1 - h), edev)
     arrived("l+1a", "l-1b")
     push("b-1", lpart(1, y, 1), lpart(1, y, 1), ydev)
+    arrived("mc+2", "mc-2")
+    push("mc+3", rc.at[6], rc.at[5], zdev(1))
+    push("mc-3", rc.at[2], rc.at[3], zdev(-1))
     hop(2, h, "o", 0)
     hop(2, h, "o", 1)
     share(2, h, "o")
-    arrived("mc+1", "mc-1", "nb+1", "nb-1")
-    push("mc+2", rc.at[7], rc.at[6], zdev(1))
-    push("mc-2", rc.at[1], rc.at[2], zdev(-1))
-    push("nb+2", lc.at[0], lc.at[1], xdev(1))
     arrived("lya")
     push("a+1", lpart(0, 1 - y, 0), lpart(0, 1 - y, 0), xdev(1))
     push("a-1", lpart(0, 1 - y, 0), lpart(0, 1 - y, 0), xdev(-1))
+    arrived("mc+3", "mc-3")
+    push("mc+4", rc.at[5], rc.at[4], zdev(1))
     hop(1, 1 - h, "p", 0)
     arrived("l+1b", "l-1a")
     push("l+2", lpart(-1, y, 0), lpart(-1, y, 0), xdev(1))
@@ -169,14 +173,9 @@
     push("b+1", lpart(-1, y, 1), lpart(-1, y, 1), ydev)
     hop(1, 1 - h, "p", 1)
     share(1, 1 - h, "p")
-    arrived("mc+2", "mc-2", "nb+2")
-    push("mc+3", rc.at[6], rc.at[5], zdev(1))
-    push("mc-3", rc.at[2], rc.at[3], zdev(-1))
     hop(3, h, "o", 0)
     hop(3, h, "o", 1)
     share(3, h, "o")
-    arrived("mc+3", "mc-3")
-    push("mc+4", rc.at[5], rc.at[4], zdev(1))
     arrived("a+1", "a-1")
     push("a+2", lpart(-1, 1 - y, 0), lpart(-1, 1 - y, 0), xdev(1))
     hop(2, 1 - h, "p", 0)
@@ -185,7 +184,7 @@
     arrived("lyb", "b-1")
     push("b-2", lpart(1, 1 - y, 1), lpart(1, 1 - y, 1), xdev(-1))
 
-    arrived("mc+4")
+    arrived("nb+2", "mc+4")
     right_table = rc[0]
     for d in range(1, NZ):
         right_table = right_table + rc[d]

time: 98.2 us -> 81.2 us (0.83); the launches traced: 98.1 us -> 80.1 us
  Pallas kernels: 95.4 us -> 77.4 us
    pallas_call x1, Pallas kernels: 95.4 us -> 77.4 us  [per_device(): pl.pallas_call(kernel, out_shape=jax.ShapeDtypeStruct((ROWS, OSLOT, BLK,...]
where the time goes in v3:
time: 81.2 us; the launch traced here: 80.1 us
  Pallas kernels  77.4 us (95%)
  local copies, waits for them, and re-layouts  2.7 us (3%)
    pallas_call x1, Pallas kernels, per_device(): pl.pallas_call(kernel, out_shape=jax.ShapeDtypeStruct((ROWS, OSLOT, BLK,...  77.4 us
    unnamed x1, local copies, waits for them, and re-layouts  2.7 us

profile of v3, /device:TPU:1, one launch (start us, length us, event | category | flops | bytes accessed | tf_op | source)
XLA Modules:
  0.0 80.1 jit_solution(7846120809431894726)
XLA Ops:
  0.0 77.4 %shard_map.82 = f32[4,6,128,128]{3,2,1,0:T(8,128)} custom-call(s32[4,8]{1,0:T(4,128)} %refs_0_.1, s32[4,4]{1,0:T(4,128)} %refs_1_.1, s32[4,3]{1,0:T(4,128)} %refs_2_.1, s32[4]{0:T(128)} %bitcast.4, s32[4,6]{1,0:T(4,128)} %refs_4_.1, s32[4]{0:T(128)} %bitcast.5, bf16[4,8,128,128]{3,2,1,0:T(8,128)(2,1)} %refs_6_.1, bf16[12,128,128]{2,1,0:T(8,128)(2,1)} %bitcast.3), custom_call_target="tpu_custom_call" | custom-call | tf_op jit(solution)/shard_map/pallas_call | solution.py:306
  77.4 2.7 %copy.10 = f32[4,6,128,128]{3,2,1,0:T(8,128)} copy(f32[4,6,128,128]{3,2,1,0:T(8,128)} %shard_map.82) | data formatting | bytes 3145728

commit v4 on v3

v4 whole, which is shorter than its diff:
```python
import functools

import jax
import jax.numpy as jnp
from jax import lax
from jax.experimental import pallas as pl
from jax.experimental.pallas import tpu as pltpu
from jax.sharding import PartitionSpec as P

MESH = pl.DeviceIdType.MESH
BLK = 128
NZ, NX = 8, 4
ROWS, LSLOT, RSLOT, OSLOT = 4, 8, 3, 6
RDEV = ROWS * RSLOT
ZERO = RDEV
PART = RDEV + 1
COPIES = 96


def kernel(*refs):
    small_in, (left, right, out, acc, lbuf), parts, rest = refs[:6], refs[6:11], refs[11:18], refs[18:]
    small, rest = rest[:6], rest[6:]
    near, next_, mid_o, mid_p, far_o, far_p, far_q = parts
    lidx, lcnt, ridx, rcnt, pidx, pcnt = small
    rm, rc, lm, ls, lc, code_v, code, lk, send, recv, local, done = rest
    row, col = lax.axis_index("row"), lax.axis_index("col")
    z, h, e = row // 4, (row // 2) % 2, row % 2
    x, y = col // 2, col % 2

    def zdev(d):
        return (((z + d) % NZ) * 4 + h * 2 + e, col)

    def xdev(d):
        return (row, ((x + d) % NX) * 2 + y)

    hdev = (z * 4 + (1 - h) * 2 + e, col)
    edev = (z * 4 + h * 2 + (1 - e), col)
    ydev = (row, x * 2 + (1 - y))

    barrier = pltpu.get_barrier_semaphore()
    partners = [zdev(1), zdev(-1), xdev(1), xdev(-1), hdev, edev, ydev]
    for dev in partners:
        pl.semaphore_signal(barrier, inc=1, device_id=dev, device_id_type=MESH)

    def rpart(d, tag, half=None):
        hh = h if tag == "o" else 1 - h
        if d in (-1, 0, 1):
            ref, at = near, (d + 1) * 4 + hh * 2 + e
        elif d in (-2, 2):
            ref, at = next_, (d + 2) + hh * 2 + e
        elif d in (-3, 3):
            ref, at = (mid_o if tag == "o" else mid_p), (d + 3) // 3 + e
        else:
            ref, at = (far_o, e) if tag == "o" else (far_p, 0)
        if half is None:
            return ref.at[pl.ds(at * PART, RDEV)]
        return ref.at[pl.ds(at * PART + half * (RDEV // 2), RDEV // 2)]

    def lpart(dx, yy, half=None):
        at = ((x + dx) % NX) * 2 + yy
        if half is None:
            return lbuf.at[at]
        return lbuf.at[at, pl.ds(2 * half, 2)]

    def lrow(dx, yy, i):
        return lbuf.at[((x + dx) % NX) * 2 + yy, pl.ds(i, 1)]

    loads = [pltpu.make_async_copy(a, b, local.at[n]) for n, (a, b) in enumerate(zip(small_in, small))]
    for load in loads:
        load.start()
    own_left = pltpu.make_async_copy(left, lpart(0, y), local.at[6])
    own_left.start()
    own_right = pltpu.make_async_copy(right, rpart(0, "o"), local.at[7])
    own_right.start()
    for load in loads:
        load.wait()

    sub = lax.broadcasted_iota(jnp.int32, (8, BLK), 0)
    lane = lax.broadcasted_iota(jnp.int32, (8, BLK), 1)
    table = jnp.zeros((8, BLK), jnp.int32)
    for j in range(ROWS):
        for t in range(RSLOT):
            value = jnp.where(t < rcnt[j], ridx[j, t] + 1, 0)
            table = jnp.where((sub == t) & (lane == row * ROWS + j), value, table)
    rm[0] = table
    table = jnp.zeros((8, BLK), jnp.int32)
    for i in range(ROWS):
        for s in range(LSLOT):
            value = jnp.where(s % 2 < lcnt[i, s // 2], (col * 4 + s // 2) * ROWS + lidx[i, s] + 1, 0)
            table = jnp.where((sub == i) & (lane == col * LSLOT + s), value, table)
    lm[0] = table

    pl.semaphore_wait(barrier, len(partners))

    copies = {}

    def push(name, src, dst, dev):
        n = len(copies)
        copy = pltpu.make_async_remote_copy(
            src_ref=src,
            dst_ref=dst,
            send_sem=send.at[n],
            recv_sem=recv.at[n],
            device_id=dev,
            device_id_type=MESH,
        )
        copy.start()
        copies[name] = copy

    def arrived(*names):
        for name in names:
            copies[name].wait_recv()

    def hop(d, tag, half):
        arrived(f"r+{d}{tag}{half}", f"r-{d}{tag}{half}")
        if d < 3 or half == 0:
            push(f"r+{d + 1}{tag}{half}", rpart(-d, tag, half), rpart(-d - 1, tag, half), zdev(1))
        if d < 3 or half == 1:
            push(f"r-{d + 1}{tag}{half}", rpart(d, tag, half), rpart(d + 1, tag, half), zdev(-1))

    def last(d, half):
        arrived(f"r+{d}p{half}", f"r-{d}p{half}")
        for n in range(2):
            at = pl.ds(6 * half + 3 * n, 3)
            way, below = ("-", 1) if half else ("+", -1)
            src = mid_p.at[pl.ds(((1 + below) + e) * PART + 6 * half + 3 * n, 3)]
            push(f"r{way}4p{n}", src, far_p.at[at], zdev(-below))

    def share(d, tag):
        push(f"e-{d}{tag}", rpart(-d, tag), rpart(-d, tag), edev)
        push(f"e+{d}{tag}", rpart(d, tag), rpart(d, tag), edev)

    def multiply(ref, d_of, devices, rows_of, write=False):
        groups = ref.shape[0] // (PART * len(devices))

        def one_group(j, carry):
            c = (z + d_of(j) + NZ) % NZ
            dx, dy = (c // 2 - x + NX) % NX, (c + y) % 2

            def one_row(i):
                slots = [(n, 2 * g + s) for n, g in enumerate(devices) for s in range(2)]
                ks = [lk[i, c * LSLOT + s] for _, s in slots]
                lhs = jnp.concatenate([lbuf[c, i, s] for _, s in slots], axis=1)
                for u in range(0, OSLOT, 2):
                    rhs = jnp.concatenate(
                        [
                            jnp.concatenate(
                                [
                                    ref[(j * len(devices) + n) * PART + code[i * OSLOT + u + v, k]]
                                    for v in range(2)
                                ],
                                axis=1,
                            )
                            for (n, _), k in zip(slots, ks)
                        ],
                        axis=0,
                    )
                    part = jnp.dot(lhs, rhs, preferred_element_type=jnp.float32)
                    acc[i, u] += part[:, :BLK]
                    acc[i, u + 1] += part[:, BLK:]
                if write:
                    pltpu.make_async_copy(acc.at[i], out.at[i], done.at[i]).start()

            def two_rows(i, carry):
                one_row(2 * i)
                one_row(2 * i + 1)
                return carry

            first, last = rows_of(dx, dy)
            lax.fori_loop(first // 2, last // 2, two_rows, 0)
            return carry

        if groups == 1:
            one_group(0, 0)
        else:
            lax.fori_loop(0, groups, one_group, 0)

    same, other, every = [h * 2, h * 2 + 1], [2 - h * 2, 3 - h * 2], range(4)
    products = {
        "near": (near, lambda j: j - 1, every),
        "next": (next_, lambda j: 4 * j - 2, every),
        "mid_o": (mid_o, lambda j: 6 * j - 3, same),
        "mid_p": (mid_p, lambda j: 6 * j - 3, other),
        "far_o": (far_o, lambda j: 4, same),
        "far_p": (far_p, lambda j: 4, [2 - h * 2 + e]),
        "far_q": (far_q, lambda j: 4, [3 - h * 2 - e]),
    }

    def rows_0(dx, dy):
        return jnp.where((dx != 2) & ((dy == 0) | (dx == 0)), 4, 0)

    def rows_2(dx, dy):
        return jnp.where(dy == 0, 4, jnp.where(dx == 2, 0, jnp.where(dx == 3, 2, 4)))

    def rows_3(dx, dy):
        return jnp.where((dx == 2) & (dy == 1), 0, 4)

    def nothing(dx, dy):
        return 0

    def everything(dx, dy):
        return 4

    def work(name, before, now, write=False):
        multiply(*products[name], lambda dx, dy: (before(dx, dy), now(dx, dy)), write)

    push("ma", rm.at[0], rm.at[1], edev)
    push("mh", rm.at[0], rm.at[2], hdev)
    push("na", lm.at[0], lm.at[1], ydev)
    for half in range(2):
        own = right.at[pl.ds(half * (RDEV // 2), RDEV // 2)]
        push(f"r+1o{half}", own, rpart(-1, "o", half), zdev(1))
        push(f"r-1o{half}", own, rpart(1, "o", half), zdev(-1))
    push("rh", right, rpart(0, "o"), hdev)
    push("l+1a", left.at[pl.ds(0, 2)], lpart(0, y, 0), xdev(1))
    push("l-1b", left.at[pl.ds(2, 2)], lpart(0, y, 1), xdev(-1))
    push("lya", left.at[pl.ds(0, 2)], lpart(0, y, 0), ydev)
    push("e0o", right, rpart(0, "o"), edev)
    arrived("mh")
    push("me", rm.at[2], rm.at[3], edev)
    arrived("na")
    ls[...] = lm[0] + lm[1]
    push("nb+1", ls, lc.at[0], xdev(1))
    push("nb-1", ls, lc.at[2], xdev(-1))
    push("l+1b", left.at[pl.ds(2, 2)], lpart(0, y, 1), xdev(1))
    push("l-1a", left.at[pl.ds(0, 2)], lpart(0, y, 0), xdev(-1))
    push("lyb", left.at[pl.ds(2, 2)], lpart(0, y, 1), ydev)
    arrived("ma", "me")
    rc[0] = rm[0] + rm[1] + rm[2] + rm[3]
    push("mc+1", rc.at[0], rc.at[7], zdev(1))
    push("mc-1", rc.at[0], rc.at[1], zdev(-1))

    hop(1, "o", 0)
    acc[...] = jnp.zeros_like(acc)
    for ref in parts:
        for n in range(ref.shape[0] // PART):
            ref[n * PART + ZERO] = jnp.zeros((BLK, BLK), jnp.bfloat16)
    code_v[:, BLK:] = jnp.full((ROWS * OSLOT, BLK), ZERO, jnp.int32)
    arrived("mc+1", "mc-1")
    push("mc+2", rc.at[7], rc.at[6], zdev(1))
    push("mc-2", rc.at[1], rc.at[2], zdev(-1))
    hop(1, "o", 1)
    share(1, "o")
    arrived("rh")
    for half in range(2):
        push(f"r+1p{half}", rpart(0, "p", half), rpart(-1, "p", half), zdev(1))
        push(f"r-1p{half}", rpart(0, "p", half), rpart(1, "p", half), zdev(-1))
    push("e0p", rpart(0, "p"), rpart(0, "p"), edev)
    arrived("mc+2", "mc-2")
    push("mc+3", rc.at[6], rc.at[5], zdev(1))
    push("mc-3", rc.at[2], rc.at[3], zdev(-1))
    hop(2, "o", 0)
    arrived("l+1a", "l-1b", "nb+1", "nb-1")
    push("nb+2", lc.at[0], lc.at[1], xdev(1))
    push("l+2", lpart(-1, y, 0), lpart(-1, y, 0), xdev(1))
    push("l-2", lpart(1, y, 1), lpart(1, y, 1), xdev(-1))
    push("b-1", lpart(1, y, 1), lpart(1, y, 1), ydev)
    hop(2, "o", 1)
    share(2, "o")
    arrived("mc+3", "mc-3")
    push("mc+4", rc.at[5], rc.at[4], zdev(1))
    hop(1, "p", 0)
    arrived("lya")
    for i in range(2):
        push(f"a+1{i}", lrow(0, 1 - y, i), lrow(0, 1 - y, i), xdev(1))
        push(f"a-1{i}", lrow(0, 1 - y, i), lrow(0, 1 - y, i), xdev(-1))
    arrived("l+1b", "l-1a")
    push("b+1", lpart(-1, y, 1), lpart(-1, y, 1), ydev)
    hop(1, "p", 1)
    share(1, "p")
    hop(3, "o", 0)
    arrived("nb+2", "mc+4")
    right_table = rc[0]
    for d in range(1, NZ):
        right_table = right_table + rc[d]
    left_table = ls[...]
    for d in range(NX - 1):
        left_table = left_table + lc[d]
    lc[NX - 1] = jnp.where(left_table == 0, BLK, left_table - 1)
    wide_sub = lax.broadcasted_iota(jnp.int32, (ROWS * OSLOT, BLK), 0)
    wide_lane = lax.broadcasted_iota(jnp.int32, (ROWS * OSLOT, BLK), 1)
    wanted = jnp.full((ROWS * OSLOT, BLK), -1, jnp.int32)
    for i in range(ROWS):
        for u in range(OSLOT):
            value = jnp.where(u < pcnt[i], pidx[i, u] + 1, -1)
            wanted = jnp.where(wide_sub == i * OSLOT + u, value, wanted)
    found = jnp.full((ROWS * OSLOT, BLK), ZERO, jnp.int32)
    for t in range(RSLOT):
        found = jnp.where(right_table[t : t + 1, :] == wanted, (wide_lane % ROWS) * RSLOT + t, found)
    code_v[:, :BLK] = found
    to_code = pltpu.make_async_copy(code_v, code, local.at[8])
    to_code.start()
    to_lk = pltpu.make_async_copy(lc.at[NX - 1], lk, local.at[9])
    to_lk.start()

    hop(3, "o", 1)
    share(3, "o")
    own_left.wait()
    own_right.wait()
    to_code.wait()
    to_lk.wait()
    for tag in "op":
        arrived(f"e0{tag}", f"e-1{tag}", f"e+1{tag}")
    arrived("lyb")
    work("near", nothing, rows_0)
    hop(2, "p", 0)
    arrived("a+10", "a-10")
    push("a+20", lrow(-1, 1 - y, 0), lrow(-1, 1 - y, 0), xdev(1))
    hop(2, "p", 1)
    share(2, "p")
    arrived("b-1")
    push("b-2", lpart(1, 1 - y, 1), lpart(1, 1 - y, 1), xdev(-1))
    for tag in "op":
        arrived(f"e-2{tag}", f"e+2{tag}")
    work("next", nothing, rows_0)
    arrived("a+11", "a-11")
    push("a+21", lrow(-1, 1 - y, 1), lrow(-1, 1 - y, 1), xdev(1))
    arrived("r+4o0", "r-4o1")
    push("e4o", rpart(4, "o"), rpart(4, "o"), edev)
    arrived("l+2", "l-2", "e-3o", "e+3o")
    work("near", rows_0, rows_2)
    work("next", rows_0, rows_2)
    last(3, 0)
    work("mid_o", nothing, rows_2)
    last(3, 1)
    share(3, "p")
    arrived("b+1", "e4o")
    for name in ("near", "next", "mid_o", "far_o"):
        work(name, rows_2 if name != "far_o" else nothing, rows_3)
    arrived("a+20", "a+21", "b-2")
    for name in ("near", "next", "mid_o", "far_o"):
        work(name, rows_3, everything)
    arrived("e-3p", "e+3p")
    work("mid_p", nothing, everything)
    arrived("r+4p0", "r-4p0")
    push("e4p0", far_p.at[pl.ds(0, 3)], far_q.at[pl.ds(0, 3)], edev)
    push("e4p1", far_p.at[pl.ds(6, 3)], far_q.at[pl.ds(6, 3)], edev)
    arrived("r+4p1", "r-4p1")
    push("e4p2", far_p.at[pl.ds(3, 3)], far_q.at[pl.ds(3, 3)], edev)
    push("e4p3", far_p.at[pl.ds(9, 3)], far_q.at[pl.ds(9, 3)], edev)
    work("far_p", nothing, everything)
    arrived("e4p0", "e4p1", "e4p2", "e4p3")
    work("far_q", nothing, everything, write=True)

    for copy in copies.values():
        copy.wait_send()
    for i in range(ROWS):
        pltpu.make_async_copy(acc.at[i], out.at[i], done.at[i]).wait()


def per_device(
    left_blocks,
    left_index,
    left_count,
    right_blocks,
    right_index,
    right_count,
    product_index,
    product_count,
):
    small = (
        left_index,
        left_count,
        right_index,
        right_count.reshape(ROWS),
        product_index,
        product_count.reshape(ROWS),
    )
    meta = functools.partial(pltpu.VMEM, dtype=jnp.int32)
    return pl.pallas_call(
        kernel,
        out_shape=jax.ShapeDtypeStruct((ROWS, OSLOT, BLK, BLK), jnp.float32),
        in_specs=[pl.BlockSpec(memory_space=pltpu.HBM)] * 8,
        out_specs=pl.BlockSpec(memory_space=pl.ANY),
        scratch_shapes=[
            pltpu.VMEM((ROWS, OSLOT, BLK, BLK), jnp.float32),
            pltpu.VMEM((8, ROWS, LSLOT, BLK, BLK), jnp.bfloat16),
        ]
        + [pltpu.VMEM((n * PART, BLK, BLK), jnp.bfloat16) for n in (12, 8, 4, 4, 2, 1, 1)]
        + [pltpu.SMEM(a.shape, jnp.int32) for a in small]
        + [
            meta((4, 8, BLK)),
            meta((NZ, 8, BLK)),
            meta((2, 8, BLK)),
            meta((8, BLK)),
            meta((NX, 8, BLK)),
            meta((ROWS * OSLOT, 2 * BLK)),
            pltpu.SMEM((ROWS * OSLOT, 2 * BLK), jnp.int32),
            pltpu.SMEM((8, BLK), jnp.int32),
            pltpu.SemaphoreType.DMA((COPIES,)),
            pltpu.SemaphoreType.DMA((COPIES,)),
            pltpu.SemaphoreType.DMA((10,)),
            pltpu.SemaphoreType.DMA((ROWS,)),
        ],
        compiler_params=pltpu.CompilerParams(
            collective_id=0, has_side_effects=True, vmem_limit_bytes=63 * 1024 * 1024
        ),
    )(*small, left_blocks, right_blocks.reshape(RDEV, BLK, BLK))


def solution(mesh):
    return jax.shard_map(
        per_device,
        mesh=mesh,
        in_specs=(
            P("row", "col", None, None),
            P("row", "col"),
            P("row", "col"),
            P("row", "col", None, None),
            P("row", "col"),
            P("row", "col"),
            P("row", "col"),
            P("row", "col"),
        ),
        out_specs=P("row", "col", None, None),
        check_vma=False,
    )
```

time: 81.2 us -> 79.2 us (0.975); the launches traced: 80.1 us -> 79 us
  Pallas kernels: 77.4 us -> 76.3 us
    pallas_call x1, Pallas kernels: 77.4 us -> 76.3 us  [per_device(): pl.pallas_call(kernel, out_shape=jax.ShapeDtypeStruct((ROWS, OSLOT, BLK,...]
where the time goes in v4:
time: 79.2 us; the launch traced here: 79 us
  Pallas kernels  76.3 us (96%)
  local copies, waits for them, and re-layouts  2.7 us (3%)
    pallas_call x1, Pallas kernels, per_device(): pl.pallas_call(kernel, out_shape=jax.ShapeDtypeStruct((ROWS, OSLOT, BLK,...  76.3 us
    unnamed x1, local copies, waits for them, and re-layouts  2.7 us

profile of v4, /device:TPU:1, one launch (start us, length us, event | category | flops | bytes accessed | tf_op | source)
XLA Modules:
  0.0 79.0 jit_solution(3430111173879825046)
XLA Ops:
  0.0 76.3 %shard_map.82 = f32[4,6,128,128]{3,2,1,0:T(8,128)} custom-call(s32[4,8]{1,0:T(4,128)} %refs_0_.1, s32[4,4]{1,0:T(4,128)} %refs_1_.1, s32[4,3]{1,0:T(4,128)} %refs_2_.1, s32[4]{0:T(128)} %bitcast.4, s32[4,6]{1,0:T(4,128)} %refs_4_.1, s32[4]{0:T(128)} %bitcast.5, bf16[4,8,128,128]{3,2,1,0:T(8,128)(2,1)} %refs_6_.1, bf16[12,128,128]{2,1,0:T(8,128)(2,1)} %bitcast.3), custom_call_target="tpu_custom_call" | custom-call | tf_op jit(solution)/shard_map/pallas_call | solution.py:370
  76.3 2.7 %copy.10 = f32[4,6,128,128]{3,2,1,0:T(8,128)} copy(f32[4,6,128,128]{3,2,1,0:T(8,128)} %shard_map.82) | data formatting | bytes 3145728

commit v5 on v4

--- a/solution.py
+++ b/solution.py
@@ -18,11 +18,11 @@
 
 
 def kernel(*refs):
-    small_in, (left, right, out, acc, lbuf), parts, rest = refs[:6], refs[6:11], refs[11:18], refs[18:]
+    small_in, (left, right, acc, lbuf), parts, rest = refs[:6], refs[6:10], refs[10:17], refs[17:]
     small, rest = rest[:6], rest[6:]
     near, next_, mid_o, mid_p, far_o, far_p, far_q = parts
     lidx, lcnt, ridx, rcnt, pidx, pcnt = small
-    rm, rc, lm, ls, lc, code_v, code, lk, send, recv, local, done = rest
+    rm, rc, lm, ls, lc, code_v, code, lk, send, recv, local = rest
     row, col = lax.axis_index("row"), lax.axis_index("col")
     z, h, e = row // 4, (row // 2) % 2, row % 2
     x, y = col // 2, col % 2
@@ -130,7 +130,7 @@
         push(f"e-{d}{tag}", rpart(-d, tag), rpart(-d, tag), edev)
         push(f"e+{d}{tag}", rpart(d, tag), rpart(d, tag), edev)
 
-    def multiply(ref, d_of, devices, rows_of, write=False):
+    def multiply(ref, d_of, devices, rows_of):
         groups = ref.shape[0] // (PART * len(devices))
 
         def one_group(j, carry):
@@ -158,8 +158,6 @@
                     part = jnp.dot(lhs, rhs, preferred_element_type=jnp.float32)
                     acc[i, u] += part[:, :BLK]
                     acc[i, u + 1] += part[:, BLK:]
-                if write:
-                    pltpu.make_async_copy(acc.at[i], out.at[i], done.at[i]).start()
 
             def two_rows(i, carry):
                 one_row(2 * i)
@@ -201,8 +199,8 @@
     def everything(dx, dy):
         return 4
 
-    def work(name, before, now, write=False):
-        multiply(*products[name], lambda dx, dy: (before(dx, dy), now(dx, dy)), write)
+    def work(name, before, now):
+        multiply(*products[name], lambda dx, dy: (before(dx, dy), now(dx, dy)))
 
     push("ma", rm.at[0], rm.at[1], edev)
     push("mh", rm.at[0], rm.at[2], hdev)
@@ -340,12 +338,10 @@
     push("e4p3", far_p.at[pl.ds(9, 3)], far_q.at[pl.ds(9, 3)], edev)
     work("far_p", nothing, everything)
     arrived("e4p0", "e4p1", "e4p2", "e4p3")
-    work("far_q", nothing, everything, write=True)
+    work("far_q", nothing, everything)
 
     for copy in copies.values():
         copy.wait_send()
-    for i in range(ROWS):
-        pltpu.make_async_copy(acc.at[i], out.at[i], done.at[i]).wait()
 
 
 def per_device(
@@ -366,14 +362,14 @@
         product_index,
         product_count.reshape(ROWS),
     )
+    operands = (*small, left_blocks, right_blocks.reshape(RDEV, BLK, BLK))
     meta = functools.partial(pltpu.VMEM, dtype=jnp.int32)
     return pl.pallas_call(
         kernel,
-        out_shape=jax.ShapeDtypeStruct((ROWS, OSLOT, BLK, BLK), jnp.float32),
-        in_specs=[pl.BlockSpec(memory_space=pltpu.HBM)] * 8,
-        out_specs=pl.BlockSpec(memory_space=pl.ANY),
+        out_shape=pltpu.VMEM((ROWS, OSLOT, BLK, BLK), jnp.float32),
+        in_specs=[pl.BlockSpec(memory_space=pl.ANY)] * 8,
+        out_specs=pl.BlockSpec(memory_space=pltpu.VMEM),
         scratch_shapes=[
-            pltpu.VMEM((ROWS, OSLOT, BLK, BLK), jnp.float32),
             pltpu.VMEM((8, ROWS, LSLOT, BLK, BLK), jnp.bfloat16),
         ]
         + [pltpu.VMEM((n * PART, BLK, BLK), jnp.bfloat16) for n in (12, 8, 4, 4, 2, 1, 1)]
@@ -390,12 +386,11 @@
             pltpu.SemaphoreType.DMA((COPIES,)),
             pltpu.SemaphoreType.DMA((COPIES,)),
             pltpu.SemaphoreType.DMA((10,)),
-            pltpu.SemaphoreType.DMA((ROWS,)),
         ],
         compiler_params=pltpu.CompilerParams(
-            collective_id=0, has_side_effects=True, vmem_limit_bytes=63 * 1024 * 1024
+            collective_id=0, has_side_effects=True, vmem_limit_bytes=48 * 1024 * 1024
         ),
-    )(*small, left_blocks, right_blocks.reshape(RDEV, BLK, BLK))
+    )(*[pltpu.with_memory_space_constraint(a, pltpu.HBM) for a in operands])
 
 
 def solution(mesh):

time: 79.2 us -> 76.8 us (0.970)
  local copies, waits for them, and re-layouts: 2.7 us -> 1.15 us
    unnamed x1, local copies, waits for them, and re-layouts: 2.7 us -> 1.15 us
where the time goes in v5:
time: 76.8 us; the launch traced here: 76.7 us
  Pallas kernels  75.6 us (98%)
  local copies, waits for them, and re-layouts  1.15 us (1%)
    pallas_call x1, Pallas kernels, per_device(): pl.pallas_call(kernel, out_shape=pltpu.VMEM((ROWS, OSLOT, BLK, BLK), jnp....  75.6 us

profile of v5, /device:TPU:1, one launch (start us, length us, event | category | flops | bytes accessed | tf_op | source)
XLA Modules:
  0.0 76.7 jit_solution(3161239891130892145)
XLA Ops:
  0.0 75.6 %shard_map.82 = f32[4,6,128,128]{3,2,1,0:T(8,128)S(1)} custom-call(s32[4,8]{1,0:T(4,128)} %refs_0_.1, s32[4,4]{1,0:T(4,128)} %refs_1_.1, s32[4,3]{1,0:T(4,128)} %refs_2_.1, s32[4]{0:T(128)} %bitcast.4, s32[4,6]{1,0:T(4,128)} %refs_4_.1, s32[4]{0:T(128)} %bitcast.5, bf16[4,8,128,128]{3,2,1,0:T(8,128)(2,1)} %refs_6_.1, bf16[12,128,128]{2,1,0:T(8,128)(2,1)} %bitcast.3), custom_call_target="tpu_custom_call" | custom-call | tf_op jit(solution)/shard_map/pallas_call | solution.py:367
  75.6 1.1 %copy.10 = f32[4,6,128,128]{3,2,1,0:T(8,128)} copy(f32[4,6,128,128]{3,2,1,0:T(8,128)S(1)} %shard_map.82) | data formatting | bytes 3145728

commit v6 on v5

--- a/solution.py
+++ b/solution.py
@@ -15,6 +15,7 @@
 ZERO = RDEV
 PART = RDEV + 1
 COPIES = 96
+TAIL = 2
 
 
 def kernel(*refs):
@@ -55,6 +56,14 @@
         if half is None:
             return ref.at[pl.ds(at * PART, RDEV)]
         return ref.at[pl.ds(at * PART + half * (RDEV // 2), RDEV // 2)]
+
+    def rtail(d, tag):
+        hh = h if tag == "o" else 1 - h
+        return near.at[pl.ds(((d + 1) * 4 + hh * 2 + e) * PART + RDEV - TAIL, TAIL)]
+
+    def rmost(d, half):
+        first = ((d + 1) * 4 + (1 - h) * 2 + e) * PART + half * (RDEV // 2)
+        return near.at[pl.ds(first, RDEV // 2 - half * TAIL)]
 
     def lpart(dx, yy, half=None):
         at = ((x + dx) % NX) * 2 + yy
@@ -222,7 +231,6 @@
     push("nb-1", ls, lc.at[2], xdev(-1))
     push("l+1b", left.at[pl.ds(2, 2)], lpart(0, y, 1), xdev(1))
     push("l-1a", left.at[pl.ds(0, 2)], lpart(0, y, 0), xdev(-1))
-    push("lyb", left.at[pl.ds(2, 2)], lpart(0, y, 1), ydev)
     arrived("ma", "me")
     rc[0] = rm[0] + rm[1] + rm[2] + rm[3]
     push("mc+1", rc.at[0], rc.at[7], zdev(1))
@@ -238,11 +246,14 @@
     push("mc+2", rc.at[7], rc.at[6], zdev(1))
     push("mc-2", rc.at[1], rc.at[2], zdev(-1))
     hop(1, "o", 1)
+    for d in (-1, 1):
+        push(f"v{d}", rtail(d, "o"), rtail(d, "o"), hdev)
+    push("lyb", left.at[pl.ds(2, 2)], lpart(0, y, 1), ydev)
     share(1, "o")
     arrived("rh")
     for half in range(2):
-        push(f"r+1p{half}", rpart(0, "p", half), rpart(-1, "p", half), zdev(1))
-        push(f"r-1p{half}", rpart(0, "p", half), rpart(1, "p", half), zdev(-1))
+        push(f"r+1p{half}", rmost(0, half), rmost(-1, half), zdev(1))
+        push(f"r-1p{half}", rmost(0, half), rmost(1, half), zdev(-1))
     push("e0p", rpart(0, "p"), rpart(0, "p"), edev)
     arrived("mc+2", "mc-2")
     push("mc+3", rc.at[6], rc.at[5], zdev(1))
@@ -264,6 +275,7 @@
         push(f"a-1{i}", lrow(0, 1 - y, i), lrow(0, 1 - y, i), xdev(-1))
     arrived("l+1b", "l-1a")
     push("b+1", lpart(-1, y, 1), lpart(-1, y, 1), ydev)
+    arrived("v-1", "v1")
     hop(1, "p", 1)
     share(1, "p")
     hop(3, "o", 0)

time: 76.8 us -> 75.4 us (0.982)
  Pallas kernels: 75.6 us -> 74.2 us
    pallas_call x1, Pallas kernels: 75.6 us -> 74.2 us  [per_device(): pl.pallas_call(kernel, out_shape=pltpu.VMEM((ROWS, OSLOT, BLK, BLK), jnp....]
where the time goes in v6:
time: 75.4 us; the launch traced here: 75.3 us
  Pallas kernels  74.2 us (98%)
  local copies, waits for them, and re-layouts  1.15 us (2%)
    pallas_call x1, Pallas kernels, per_device(): pl.pallas_call(kernel, out_shape=pltpu.VMEM((ROWS, OSLOT, BLK, BLK), jnp....  74.2 us

profile of v6, /device:TPU:1, one launch (start us, length us, event | category | flops | bytes accessed | tf_op | source)
XLA Modules:
  0.0 75.3 jit_solution(2982903346093860416)
XLA Ops:
  0.0 74.2 %shard_map.82 = f32[4,6,128,128]{3,2,1,0:T(8,128)S(1)} custom-call(s32[4,8]{1,0:T(4,128)} %refs_0_.1, s32[4,4]{1,0:T(4,128)} %refs_1_.1, s32[4,3]{1,0:T(4,128)} %refs_2_.1, s32[4]{0:T(128)} %bitcast.4, s32[4,6]{1,0:T(4,128)} %refs_4_.1, s32[4]{0:T(128)} %bitcast.5, bf16[4,8,128,128]{3,2,1,0:T(8,128)(2,1)} %refs_6_.1, bf16[12,128,128]{2,1,0:T(8,128)(2,1)} %bitcast.3), custom_call_target="tpu_custom_call" | custom-call | tf_op jit(solution)/shard_map/pallas_call | solution.py:379
  74.2 1.1 %copy.10 = f32[4,6,128,128]{3,2,1,0:T(8,128)} copy(f32[4,6,128,128]{3,2,1,0:T(8,128)S(1)} %shard_map.82) | data formatting | bytes 3145728

commit v7 on v6

--- a/solution.py
+++ b/solution.py
@@ -337,18 +337,18 @@
     arrived("b+1", "e4o")
     for name in ("near", "next", "mid_o", "far_o"):
         work(name, rows_2 if name != "far_o" else nothing, rows_3)
-    arrived("a+20", "a+21", "b-2")
-    for name in ("near", "next", "mid_o", "far_o"):
-        work(name, rows_3, everything)
     arrived("e-3p", "e+3p")
-    work("mid_p", nothing, everything)
+    work("mid_p", nothing, rows_3)
     arrived("r+4p0", "r-4p0")
     push("e4p0", far_p.at[pl.ds(0, 3)], far_q.at[pl.ds(0, 3)], edev)
     push("e4p1", far_p.at[pl.ds(6, 3)], far_q.at[pl.ds(6, 3)], edev)
     arrived("r+4p1", "r-4p1")
     push("e4p2", far_p.at[pl.ds(3, 3)], far_q.at[pl.ds(3, 3)], edev)
     push("e4p3", far_p.at[pl.ds(9, 3)], far_q.at[pl.ds(9, 3)], edev)
-    work("far_p", nothing, everything)
+    work("far_p", nothing, rows_3)
+    arrived("a+20", "a+21", "b-2")
+    for name in ("near", "next", "mid_o", "mid_p", "far_o", "far_p"):
+        work(name, rows_3, everything)
     arrived("e4p0", "e4p1", "e4p2", "e4p3")
     work("far_q", nothing, everything)
 

time: 75.4 us -> 75 us (level)
  no operation moved by 1% of the time
where the time goes in v7:
time: 75 us; the launch traced here: 74.9 us
  Pallas kernels  73.7 us (98%)
  local copies, waits for them, and re-layouts  1.15 us (2%)
    pallas_call x1, Pallas kernels, per_device(): pl.pallas_call(kernel, out_shape=pltpu.VMEM((ROWS, OSLOT, BLK, BLK), jnp....  73.7 us

profile of v7, /device:TPU:1, one launch (start us, length us, event | category | flops | bytes accessed | tf_op | source)
XLA Modules:
  0.0 74.9 jit_solution(13295823620045344223)
XLA Ops:
  0.0 73.7 %shard_map.82 = f32[4,6,128,128]{3,2,1,0:T(8,128)S(1)} custom-call(s32[4,8]{1,0:T(4,128)} %refs_0_.1, s32[4,4]{1,0:T(4,128)} %refs_1_.1, s32[4,3]{1,0:T(4,128)} %refs_2_.1, s32[4]{0:T(128)} %bitcast.4, s32[4,6]{1,0:T(4,128)} %refs_4_.1, s32[4]{0:T(128)} %bitcast.5, bf16[4,8,128,128]{3,2,1,0:T(8,128)(2,1)} %refs_6_.1, bf16[12,128,128]{2,1,0:T(8,128)(2,1)} %bitcast.3), custom_call_target="tpu_custom_call" | custom-call | tf_op jit(solution)/shard_map/pallas_call | solution.py:379
  73.7 1.1 %copy.10 = f32[4,6,128,128]{3,2,1,0:T(8,128)} copy(f32[4,6,128,128]{3,2,1,0:T(8,128)S(1)} %shard_map.82) | data formatting | bytes 3145728

commit v8 on v7

--- a/solution.py
+++ b/solution.py
@@ -81,24 +81,6 @@
     own_left.start()
     own_right = pltpu.make_async_copy(right, rpart(0, "o"), local.at[7])
     own_right.start()
-    for load in loads:
-        load.wait()
-
-    sub = lax.broadcasted_iota(jnp.int32, (8, BLK), 0)
-    lane = lax.broadcasted_iota(jnp.int32, (8, BLK), 1)
-    table = jnp.zeros((8, BLK), jnp.int32)
-    for j in range(ROWS):
-        for t in range(RSLOT):
-            value = jnp.where(t < rcnt[j], ridx[j, t] + 1, 0)
-            table = jnp.where((sub == t) & (lane == row * ROWS + j), value, table)
-    rm[0] = table
-    table = jnp.zeros((8, BLK), jnp.int32)
-    for i in range(ROWS):
-        for s in range(LSLOT):
-            value = jnp.where(s % 2 < lcnt[i, s // 2], (col * 4 + s // 2) * ROWS + lidx[i, s] + 1, 0)
-            table = jnp.where((sub == i) & (lane == col * LSLOT + s), value, table)
-    lm[0] = table
-
     pl.semaphore_wait(barrier, len(partners))
 
     copies = {}
@@ -211,16 +193,35 @@
     def work(name, before, now):
         multiply(*products[name], lambda dx, dy: (before(dx, dy), now(dx, dy)))
 
-    push("ma", rm.at[0], rm.at[1], edev)
-    push("mh", rm.at[0], rm.at[2], hdev)
-    push("na", lm.at[0], lm.at[1], ydev)
     for half in range(2):
         own = right.at[pl.ds(half * (RDEV // 2), RDEV // 2)]
         push(f"r+1o{half}", own, rpart(-1, "o", half), zdev(1))
         push(f"r-1o{half}", own, rpart(1, "o", half), zdev(-1))
-    push("rh", right, rpart(0, "o"), hdev)
     push("l+1a", left.at[pl.ds(0, 2)], lpart(0, y, 0), xdev(1))
     push("l-1b", left.at[pl.ds(2, 2)], lpart(0, y, 1), xdev(-1))
+
+    for load in loads:
+        load.wait()
+
+    sub = lax.broadcasted_iota(jnp.int32, (8, BLK), 0)
+    lane = lax.broadcasted_iota(jnp.int32, (8, BLK), 1)
+    table = jnp.zeros((8, BLK), jnp.int32)
+    for j in range(ROWS):
+        for t in range(RSLOT):
+            value = jnp.where(t < rcnt[j], ridx[j, t] + 1, 0)
+            table = jnp.where((sub == t) & (lane == row * ROWS + j), value, table)
+    rm[0] = table
+    table = jnp.zeros((8, BLK), jnp.int32)
+    for i in range(ROWS):
+        for s in range(LSLOT):
+            value = jnp.where(s % 2 < lcnt[i, s // 2], (col * 4 + s // 2) * ROWS + lidx[i, s] + 1, 0)
+            table = jnp.where((sub == i) & (lane == col * LSLOT + s), value, table)
+    lm[0] = table
+
+    push("ma", rm.at[0], rm.at[1], edev)
+    push("mh", rm.at[0], rm.at[2], hdev)
+    push("na", lm.at[0], lm.at[1], ydev)
+    push("rh", right, rpart(0, "o"), hdev)
     push("lya", left.at[pl.ds(0, 2)], lpart(0, y, 0), ydev)
     push("e0o", right, rpart(0, "o"), edev)
     arrived("mh")

time: 75 us -> 74.9 us (level)
  no operation moved by 1% of the time
where the time goes in v8:
time: 74.9 us
  Pallas kernels  73.7 us (98%)
  local copies, waits for them, and re-layouts  1.15 us (2%)
    pallas_call x1, Pallas kernels, per_device(): pl.pallas_call(kernel, out_shape=pltpu.VMEM((ROWS, OSLOT, BLK, BLK), jnp....  73.7 us

profile of v8, /device:TPU:1, one launch (start us, length us, event | category | flops | bytes accessed | tf_op | source)
XLA Modules:
  0.0 74.9 jit_solution(3041562111486781031)
XLA Ops:
  0.0 73.7 %shard_map.82 = f32[4,6,128,128]{3,2,1,0:T(8,128)S(1)} custom-call(s32[4,8]{1,0:T(4,128)} %refs_0_.1, s32[4,4]{1,0:T(4,128)} %refs_1_.1, s32[4,3]{1,0:T(4,128)} %refs_2_.1, s32[4]{0:T(128)} %bitcast.4, s32[4,6]{1,0:T(4,128)} %refs_4_.1, s32[4]{0:T(128)} %bitcast.5, bf16[4,8,128,128]{3,2,1,0:T(8,128)(2,1)} %refs_6_.1, bf16[12,128,128]{2,1,0:T(8,128)(2,1)} %bitcast.3), custom_call_target="tpu_custom_call" | custom-call | tf_op jit(solution)/shard_map/pallas_call | solution.py:380
  73.7 1.1 %copy.10 = f32[4,6,128,128]{3,2,1,0:T(8,128)} copy(f32[4,6,128,128]{3,2,1,0:T(8,128)S(1)} %shard_map.82) | data formatting | bytes 3145728
